TPU v7x, 128 devices: a whole 4x4x4 slice. The times are simulated.
128 devices in a mesh: rep: 8 (over z, x_hi), tp: 16 (over y, x_lo, core).
Axes of the slice: x: 4 (x_hi: 2, x_lo: 2; x = x_hi * 2 + x_lo), y: 4, z: 4, core: 2. Of those that a mesh axis runs over, the one named last changes fastest.
Arguments:
- tokens: bfloat16 [4096, 4096], P('rep', 'tp'), may hold values from -0.078125 to 0.078125
- noise: bfloat16 [8, 4096, 11008], P('rep', None, 'tp'), may hold values from -5 to 5
- cotangent: bfloat16 [4096, 11008], P('rep', 'tp'), may hold values from -30 to 30
- mean: float32 [4096, 11008], P('rep', 'tp'), may hold values from -5 to 5
- hess: float32 [4096, 11008], P('rep', 'tp'), may hold values from 0.5 to 2
- momentum: float32 [4096, 11008], P('rep', 'tp'), may hold values from -2 to 2
Outputs:
- new_mean: float32 [4096, 11008], P('rep', 'tp')
- new_hess: float32 [4096, 11008], P('rep', 'tp')
- new_momentum: float32 [4096, 11008], P('rep', 'tp')
- input_grad: bfloat16 [4096, 4096], P(('rep', 'tp'))
All inputs are finite; a program needn't handle non-finite values.
Results may differ from a plain program's by a relative error of at most 0.007.
Values may be sent and summed in bfloat16 or wider, within the bound.
A program may use at most 128 MiB of HBM per device.

v0:
```python
import jax
import jax.numpy as jnp
from jax import lax
from jax.sharding import PartitionSpec as P


def shards(tokens, noise, cotangent, mean, hess, momentum):
    n_rep = lax.axis_size("rep")
    sigma_own = lax.rsqrt(4.0 * (hess + 0.001)).astype(jnp.bfloat16)
    mean_low = mean.astype(jnp.bfloat16)
    mean_all, sigma_all = (
        lax.all_gather(mean_low, "rep", axis=0, tiled=True),
        lax.all_gather(sigma_own, "rep", axis=0, tiled=True),
    )
    eps = noise[0]
    weight = (
        mean_all.astype(jnp.float32) + sigma_all.astype(jnp.float32) * eps.astype(jnp.float32)
    ).astype(jnp.bfloat16)
    feats = lax.all_gather(tokens, "tp", axis=1, tiled=True)
    pre = jnp.dot(feats, weight, preferred_element_type=jnp.float32)
    sig = jax.nn.sigmoid(pre)
    dpre = (cotangent.astype(jnp.float32) * sig * (1.0 + pre * (1.0 - sig))).astype(jnp.bfloat16)
    input_grad = lax.psum_scatter(
        lax.dot_general(dpre, weight, (((1,), (1,)), ((), ())), preferred_element_type=jnp.float32),
        "tp",
        scatter_dimension=0,
        tiled=True,
    ).astype(jnp.bfloat16)
    grad = lax.dot_general(
        feats, dpre, (((0,), (0,)), ((), ())), preferred_element_type=jnp.float32
    )
    hest = grad * eps.astype(jnp.float32) / sigma_all.astype(jnp.float32)
    grad_sum, hest_sum = (
        lax.psum_scatter(grad.astype(jnp.bfloat16), "rep", scatter_dimension=0, tiled=True).astype(
            jnp.float32
        ),
        lax.psum_scatter(hest.astype(jnp.bfloat16), "rep", scatter_dimension=0, tiled=True).astype(
            jnp.float32
        ),
    )
    grad_mean = grad_sum / n_rep
    hess_mean = hest_sum / n_rep
    new_momentum = 0.9 * momentum + 0.1 * grad_mean
    diff = hess - hess_mean
    new_hess = hess + 0.2 * (hess_mean - hess) + 0.5 * 0.04 * diff * diff / (hess + 0.001)
    new_mean = mean - 0.5 * (new_momentum + 0.001 * mean) / (new_hess + 0.001)
    return (new_mean, new_hess, new_momentum, input_grad)


def solution(mesh):
    in_specs = (
        P("rep", "tp"),
        P("rep", None, "tp"),
        P("rep", "tp"),
        P("rep", "tp"),
        P("rep", "tp"),
        P("rep", "tp"),
    )
    out_specs = (P("rep", "tp"), P("rep", "tp"), P("rep", "tp"), P(("rep", "tp"), None))
    return jax.shard_map(shards, mesh=mesh, in_specs=in_specs, out_specs=out_specs, check_vma=False)
```

profile of v0, /device:TPU:0, one launch (start us, length us, event | category | flops | bytes accessed | tf_op | source)
XLA Modules:
  0.0 554.5 jit_solution(2851411084683728865)
XLA Ops:
  7.2 0.0 all-gather.8.cloned.1.call-start
  7.2 0.7 all-gather.8.cloned.1.call-update
  7.9 0.0 all-gather.4.cloned.1.call-start
  8.0 2.4 convert_element_type.45
  10.3 0.0 all-gather.4.cloned.1.call-update
  10.4 0.0 all-gather.6.cloned.1.call-start
  10.4 1.0 rsqrt_convert_fusion
  11.5 0.0 reduce-scatter.6.cloned.1.call-start
  11.6 45.7 %all-gather.8.cloned.1.call-done = bf16[512,4096]{1,0:T(8,128)(2,1)} async-done(((bf16[512,256]{1,0:T(8,128)(2,1)}), bf16[512,4096]{1,0:T(8,128)(2,1)}) %all-gather.8.cloned.1.call-update) | async-done | bytes 4194320 | tf_op jit(solution)/shard_map/all_gather | solution.py:19
  57.3 90.3 %all-gather.4.cloned.1.call-done = bf16[4096,688]{0,1:T(8,128)(2,1)} async-done(((bf16[512,688]{0,1:T(8,128)(2,1)}), bf16[4096,688]{0,1:T(8,128)(2,1)}) %all-gather.4.cloned.1.call-update) | async-done | bytes 5636112 | tf_op jit(solution)/shard_map/all_gather | solution.py:12
  147.6 88.0 %all-gather.6.cloned.1.call-done = bf16[4096,688]{0,1:T(8,128)(2,1)} async-done(((bf16[512,688]{0,1:T(8,128)(2,1)}), bf16[4096,688]{0,1:T(8,128)(2,1)}) %all-gather.6.cloned.1.call-update) | async-done | bytes 5636112 | tf_op jit(solution)/shard_map/all_gather | solution.py:13
  235.6 10.1 %convolution_bitcast_fusion = f32[512,688]{0,1:T(8,128)S(1)} fusion(bf16[512,4096]{1,0:T(8,128)(2,1)} %all-gather.8.cloned.1.call-done, bf16[4096,688]{0,1:T(8,128)(2,1)} %all-gather.6.cloned.1.call-done, bf16[4096,688]{0,1:T(8,128)(2,1)} %all-gather.4.cloned.1.call-done, bf16[1,4096,688]{1,2,0:T(8,128)(2,1)} %param.7), kind=kOutput, calls=%fused_computation.8 | convolution fusion | flops 2902589440 | bytes 22511616 | tf_op jit(solution)/shard_map/dot_general | solution.py:20
  245.7 5.3 bitcast_convert_fusion
  251.1 7.5 %fusion = bf16[4096,688]{0,1:T(8,128)(2,1)} fusion(bf16[4096,688]{0,1:T(8,128)(2,1)S(1)} %copy-done, f32[688,4096]{1,0:T(8,128)S(1)} %get-tuple-element.8, bf16[1,4096,688]{1,2,0:T(8,128)(2,1)} %param.7), kind=kLoop, calls=%fused_computation.3 | loop fusion | flops 14090240 | bytes 28180480 | tf_op jit(solution)/shard_map/convert_element_type | solution.py:37
  258.6 0.0 reduce-scatter.4.cloned.1.call-start
  258.7 0.5 reduce-scatter.4.cloned.1.call-update
  259.2 0.0 reduce-scatter.8.cloned.1.call-start
  259.2 14.1 %fusion.5 = f32[512,4096]{1,0:T(8,128)} fusion(f32[512,688]{0,1:T(8,128)S(1)} %convolution_bitcast_fusion, bf16[512,688]{0,1:T(8,128)(2,1)S(1)} %copy-done.4, bf16[4096,688]{0,1:T(8,128)(2,1)} %all-gather.6.cloned.1.call-done, bf16[4096,688]{0,1:T(8,128)(2,1)} %all-gather.4.cloned.1.call-done, bf16[1,4096,688]{1,2,0:T(8,128)(2,1)} %param.7), kind=kOutput, calls=%fused_computation.14 | convolution fusion | flops 2906112000 | bytes 27410432 | tf_op jit(solution)/shard_map/dot_general | solution.py:24
  273.4 0.0 reduce-scatter.8.cloned.1.call-update
  273.4 77.4 %reduce-scatter.6.cloned.1.call-done = bf16[512,688]{0,1:T(8,128)(2,1)} async-done(((bf16[4096,688]{0,1:T(8,128)(2,1)}), bf16[512,688]{0,1:T(8,128)(2,1)}) %reduce-scatter.6.cloned.1.call-update) | async-done | bytes 704528 | tf_op jit(solution)/shard_map/reduce_scatter | solution.py:37
  350.8 96.5 %reduce-scatter.4.cloned.1.call-done = bf16[512,688]{0,1:T(8,128)(2,1)} async-done(((bf16[4096,688]{0,1:T(8,128)(2,1)}), bf16[512,688]{0,1:T(8,128)(2,1)}) %reduce-scatter.4.cloned.1.call-update) | async-done | bytes 704528 | tf_op jit(solution)/shard_map/reduce_scatter | solution.py:34
  447.2 4.4 divide_subtract_fusion
  451.6 94.3 %reduce-scatter.8.cloned.1.call-done = f32[32,4096]{1,0:T(8,128)} async-done(((f32[512,4096]{1,0:T(8,128)}), f32[32,4096]{1,0:T(8,128)}) %reduce-scatter.8.cloned.1.call-update) | async-done | bytes 524304 | tf_op jit(solution)/shard_map/reduce_scatter | solution.py:23
  545.9 1.8 convert_element_type.57
  (12 shorter events, 0.1 us)
Async XLA Ops:
  7.2 50.1 %all-gather.8.cloned.1.call-start = ((), (), s32[]{:S(2)}) async-start(), calls=%async_computation.5 | async-start | bytes 4456448 | tf_op jit(solution)/shard_map/all_gather | solution.py:19
  7.9 2.5 copy-start.2
  7.9 139.7 %all-gather.4.cloned.1.call-start = ((), (), s32[]{:S(2)}) async-start(), calls=%async_computation.3 | async-start | bytes 6340608 | tf_op jit(solution)/shard_map/all_gather | solution.py:12
  10.4 225.2 %all-gather.6.cloned.1.call-start = ((), (), s32[]{:S(2)}) async-start(), calls=%async_computation.4 | async-start | bytes 6340608 | tf_op jit(solution)/shard_map/all_gather | solution.py:13
  11.5 234.2 %copy-start.4 = (bf16[512,688]{0,1:T(8,128)(2,1)S(1)}, bf16[512,688]{0,1:T(8,128)(2,1)}, u32[]{:S(2)}) copy-start(bf16[512,688]{0,1:T(8,128)(2,1)} %param.8) | copy-start | bytes 2113540
  11.5 339.2 %reduce-scatter.6.cloned.1.call-start = ((), (), s32[]{:S(2)}) async-start(), calls=%async_computation.7 | async-start | bytes 6340608 | tf_op jit(solution)/shard_map/reduce_scatter | solution.py:37
  235.6 10.1 %copy-start.3 = (bf16[512,4096]{1,0:T(8,128)(2,1)S(1)}, bf16[512,4096]{1,0:T(8,128)(2,1)}, u32[]{:S(2)}) copy-start(bf16[512,4096]{1,0:T(8,128)(2,1)} %all-gather.8.cloned.1.call-done) | copy-start | bytes 12582916
  245.7 5.4 copy-start
  258.6 188.6 %reduce-scatter.4.cloned.1.call-start = ((), (), s32[]{:S(2)}) async-start(), calls=%async_computation.6 | async-start | bytes 6340608 | tf_op jit(solution)/shard_map/reduce_scatter | solution.py:34
  259.2 286.7 %reduce-scatter.8.cloned.1.call-start = ((), (), s32[]{:S(2)}) async-start(), calls=%async_computation.8 | async-start | bytes 8912896 | tf_op jit(solution)/shard_map/reduce_scatter | solution.py:23
  273.4 173.8 %copy-start.1 = (f32[512,688]{0,1:T(8,128)S(1)}, f32[512,688]{0,1:T(8,128)}, u32[]{:S(2)}) copy-start(f32[512,688]{0,1:T(8,128)} %param.9) | copy-start | bytes 4227076
Sparse Core Ops, SparseCore 0:
  9.6 47.6 all-gather.7
  60.0 87.4 all-gather.3
  150.3 85.2 all-gather.5
  258.7 91.9 reduce-scatter.5
  354.5 92.6 reduce-scatter.3
  449.5 96.3 reduce-scatter.7
where the time goes:
time: 555 us; the launch traced here: 554 us
  waiting for transfers between devices  493 us (89%)
  matrix products  29.6 us (5%)
  other arithmetic  17.1 us (3%)
  between operations  14.2 us (3%)
    reduce_scatter x1, waiting for transfers between devices, shards(): lax.psum_scatter(grad.astype(jnp.bfloat16), 'rep', scatter_dimension=0, t...  96.5 us
    reduce_scatter x1, waiting for transfers between devices, shards(): lax.psum_scatter(lax.dot_general(dpre, weight, (((1,), (1,)), ((), ())),...  94.3 us
    all_gather x1, waiting for transfers between devices, shards(): lax.all_gather(mean_low, 'rep', axis=0, tiled=True)  90.3 us
    all_gather x1, waiting for transfers between devices, shards(): lax.all_gather(sigma_own, 'rep', axis=0, tiled=True)  88 us
    reduce_scatter x1, waiting for transfers between devices, shards(): lax.psum_scatter(hest.astype(jnp.bfloat16), 'rep', scatter_dimension=0, t...  77.4 us
    all_gather x1, waiting for transfers between devices, shards(): feats = lax.all_gather(tokens, 'tp', axis=1, tiled=True)  45.7 us
    dot_general x1, matrix products, shards(): lax.dot_general(dpre, weight, (((1,), (1,)), ((), ())), preferred_element...  14.1 us
  transfers between devices with their start and end apart: 6, of which 6 were waited for; matrix products, arithmetic and copies ran while one was open for 4% of the time, Pallas kernels for 0%

commit v1 on v0

v1 whole, which is shorter than its diff:
```python
import functools

import jax
import jax.numpy as jnp
from jax import lax
from jax.experimental import pallas as pl
from jax.experimental.pallas import tpu as pltpu
from jax.sharding import PartitionSpec as P

MESH = pl.DeviceIdType.MESH
BF, F32 = jnp.bfloat16, jnp.float32

NZ, NY = 4, 4
UNITS, BLOCK, WIDE = 688, 512, 2048
HALF = 256
CHUNKS = ((0, 256), (256, 256), (512, 128), (640, 48))
EARLY = 2
PIECES = 2
PW = WIDE // PIECES
N_SEM = 128


def kernel(
    tok_in, noise_in, cot_in, mean_in, hess_in,
    sums_out, din_out,
    tok, tokt, n_own, n_par, ms, wt, cot, mean_v, hess_v,
    pre_own, p_send, p_recv, dp, dpt,
    g_send, g_recv, g_own, sums,
    c_send, c_recv, c_own, y_send, y_recv, y_own, l_send, l_recv, l_own, o_send, o_buf,
    ssem, rsem, lsem,
):
    rep, tp = lax.axis_index("rep"), lax.axis_index("tp")
    z, h = rep // 2, rep % 2
    y, l, c = tp // 4, (tp // 2) % 2, tp % 2

    def at(z=z, h=h, y=y, l=l, c=c):
        return (z * 2 + h, (y * 2 + l) * 2 + c)

    def zz(k):
        return lax.rem(z + k, NZ)

    def yy(k):
        return lax.rem(y + k, NY)

    partner, other_core, other_l = at(h=1 - h), at(c=1 - c), at(l=1 - l)

    def lanes(index, width, base=0):
        return pl.ds(pl.multiple_of(index * width + base, width if base == 0 else 256), width)

    count = [2]

    def remote(src, dst, device, slot=None, rslot=None):
        if slot is None:
            slot = count[0]
            count[0] += 1
        return pltpu.make_async_remote_copy(
            src_ref=src, dst_ref=dst, send_sem=ssem.at[slot], recv_sem=rsem.at[slot if rslot is None else rslot],
            device_id=device, device_id_type=MESH,
        )

    sent = []

    def send(*args, **kw):
        copy = remote(*args, **kw)
        copy.start()
        sent.append(copy)
        return copy

    peers = [other_l, partner, at(h=1 - h, l=1 - l), other_core]
    peers += [at(z=zz(k)) for k in (1, 2, 3)] + [at(y=yy(k)) for k in (1, 2, 3)]
    barrier = pltpu.get_barrier_semaphore()
    for peer in peers:
        pl.semaphore_signal(barrier, inc=1, device_id=peer, device_id_type=MESH)

    load_mean = pltpu.make_async_copy(mean_in, mean_v, lsem.at[0])
    load_hess = pltpu.make_async_copy(hess_in, hess_v, lsem.at[1])
    load_mean.start()
    load_hess.start()
    pl.semaphore_wait(barrier, len(peers))

    mine = lanes(y, 512, c * 256) if False else pl.ds(pl.multiple_of(y * 512 + c * 256, 256), 256)
    t_slot = tok.at[h, :, mine]
    t_near = remote(tok_in, t_slot, at(h=l, l=1 - l), slot=0, rslot=h)
    t_near.start()
    t_far = remote(tok_in, t_slot, partner, slot=1, rslot=h)
    t_self = pltpu.make_async_copy(tok_in, t_slot, rsem.at[h])
    stays = h == l

    @pl.when(stays)
    def _():
        t_self.start()

    @pl.when(jnp.logical_not(stays))
    def _():
        t_far.start()

    noise_copies = []

    def send_noise(k):
        first, rows = CHUNKS[k]
        noise_copies.append([
            send(
                noise_in.at[pl.ds(first, rows), pl.ds(pl.multiple_of((2 * b + 1 - h) * BLOCK, BLOCK), BLOCK)],
                n_par.at[pl.ds(first, rows), pl.ds(b * BLOCK, BLOCK)],
                partner,
            )
            for b in range(NZ)
        ])

    for k in range(EARLY):
        send_noise(k)

    load_own = []
    for b in range(NZ):
        load_own.append(
            pltpu.make_async_copy(
                noise_in.at[:, pl.ds(pl.multiple_of((2 * b + h) * BLOCK, BLOCK), BLOCK)],
                n_own.at[:, pl.ds(b * BLOCK, BLOCK)],
                lsem.at[3 + b],
            )
        )
        load_own[-1].start()
    load_cot = pltpu.make_async_copy(cot_in, cot, lsem.at[2])
    load_cot.start()

    load_mean.wait()
    load_hess.wait()
    own_z = pl.ds(pl.multiple_of(z * BLOCK, BLOCK), BLOCK)
    state_copies = []
    for first, rows in CHUNKS:

        @pl.loop(0, rows // 16)
        def _(i, first=first):
            r = pl.ds(pl.multiple_of(first + i * 16, 16), 16)
            ms[0, r, own_z] = mean_v[r, :].astype(BF)
            ms[1, r, own_z] = lax.rsqrt(4.0 * (hess_v[r, :] + 0.001)).astype(BF)

        part = ms.at[:, pl.ds(first, rows), own_z]
        state_copies.append([send(part, part, at(z=zz(k))) for k in (1, 3, 2)])

    for s in range(2):
        pltpu.make_async_copy(t_slot, tok.at[s, :, mine], rsem.at[s]).wait()
    block = tok.at[:, :, mine]
    y_copies = [send(block, block, at(y=yy(k))) for k in (1, 3, 2)]
    core_copies = [send(block, block, other_core)]
    for k, copy in zip((1, 3, 2), y_copies):
        copy.wait_recv()
        there = tok.at[:, :, pl.ds(pl.multiple_of(yy(4 - k) * 512 + c * 256, 256), 256)]
        core_copies.append(send(there, there, other_core))
    for copy in core_copies:
        copy.wait_recv()

    @pl.loop(0, 2 * WIDE // 256)
    def _(i):
        s, b = i // 8, i % 8
        f = pl.ds(pl.multiple_of(b * 256, 256), 256)
        tokt[s, f, :] = tok[s, :, f].T

    p_copies, d_copies, g_copies = {}, {}, {}
    sides = (h, 1 - h)

    def weights_and_pre(k):
        first, rows = CHUNKS[k]
        span = pl.ds(first, rows)
        for copy in state_copies[k] + noise_copies[k]:
            copy.wait_recv()

        @pl.loop(0, rows // 16)
        def _(i):
            r = pl.ds(pl.multiple_of(first + i * 16, 16), 16)
            for b in range(NZ):
                f = pl.ds(b * BLOCK, BLOCK)
                m, g = ms[0, r, f].astype(F32), ms[1, r, f].astype(F32)
                wt[0, r, f] = (m + g * n_own[r, f].astype(F32)).astype(BF)
                wt[1, r, f] = (m + g * n_par[r, f].astype(F32)).astype(BF)

        for half in range(2):
            t = pl.ds(half * HALF, HALF)
            p_send[span, t] = jnp.dot(
                wt[1, span, :], tokt[sides[1], :, t], preferred_element_type=F32
            ).astype(BF)
        p_copies[k] = send(p_send.at[span], p_recv.at[span], partner)
        for half in range(2):
            t = pl.ds(half * HALF, HALF)
            pre_own[span, t] = jnp.dot(wt[0, span, :], tokt[sides[0], :, t], preferred_element_type=F32)

    def dpre(k):
        first, rows = CHUNKS[k]
        span = pl.ds(first, rows)
        p_copies[k].wait_recv()

        @pl.loop(0, rows // 16)
        def _(i):
            r = pl.ds(pl.multiple_of(first + i * 16, 16), 16)
            pre = pre_own[r, :] + p_recv[r, :].astype(F32)
            sig = 1.0 / (1.0 + jnp.exp(-pre))
            dp[0, r, :] = (cot[r, :].astype(F32) * sig * (1.0 + pre * (1.0 - sig))).astype(BF)

        d_copies[k] = send(dp.at[0, span], dp.at[1, span], partner)
        turn(0, k)

    def turn(s, k):
        first, rows = CHUNKS[k]
        span = pl.ds(first, rows)
        for t in range(16):
            if t % 4 == 0:
                turned = dp[s, span, t * 32 : t * 32 + 128].T
            dpt[s, t % 2, pl.ds(t // 2 * 32, 32), span] = turned[t % 4 * 32 : t % 4 * 32 + 32, :]

    def grads(k):
        first, rows = CHUNKS[k]
        span = pl.ds(first, rows)
        g_copies[k] = []
        for step in (2, 1, 3, 0):
            for half in range(2):
                t = pl.ds(half * HALF, HALF)
                f = pl.ds(pl.multiple_of(zz(step) * BLOCK + half * HALF, HALF), HALF)
                one = jnp.dot(dp[0, span, :], tok[sides[0], :, f], preferred_element_type=F32)
                two = jnp.dot(dp[1, span, :], tok[sides[1], :, f], preferred_element_type=F32)
                hest = one * n_own[span, f].astype(F32) + two * n_par[span, f].astype(F32)
                if step:
                    g_send[step - 1, 0, span, t] = (one + two).astype(BF)
                    g_send[step - 1, 1, span, t] = hest.astype(BF)
                else:
                    g_own[0, span, t] = one + two
                    g_own[1, span, t] = hest
            if step:
                g_copies[k].append(
                    send(g_send.at[step - 1, :, span], g_recv.at[step - 1, :, span], at(z=zz(step)))
                )

    out_copies = []

    def finish_sums(k):
        first, rows = CHUNKS[k]
        span = pl.ds(first, rows)
        for copy in g_copies[k]:
            copy.wait_recv()

        @pl.loop(0, rows // 16)
        def _(i):
            r = pl.ds(pl.multiple_of(first + i * 16, 16), 16)
            total = [
                g_own[j, r, :]
                + (g_recv[0, j, r, :].astype(F32) + g_recv[1, j, r, :].astype(F32) + g_recv[2, j, r, :].astype(F32))
                for j in range(2)
            ]
            sums[0, r, :] = total[0]
            sums[1, r, :] = total[1] / ms[1, r, own_z].astype(F32)

        copy = pltpu.make_async_copy(sums.at[:, span], sums_out.at[:, span], lsem.at[7 + k])
        copy.start()
        out_copies.append(copy)

    c_copies, y_sends, l_copies, o_copies = {}, {}, {}, []

    def din_product(s, p):
        for which in (1 - c, c):
            for q in range(PW // HALF):
                f = pl.ds(p * PW + q * HALF, HALF)
                part = jnp.dot(dpt[s, which], wt[s, :, f], preferred_element_type=F32)
                if which is c:
                    c_own[s, :, f] = part
                else:
                    c_send[s, :, f] = part.astype(BF)
            if which is not c:
                f = pl.ds(p * PW, PW)
                c_copies[s, p] = send(c_send.at[s, :, f], c_recv.at[s, :, f], other_core)

    def din_y(s, p):
        c_copies[s, p].wait_recv()
        f = pl.ds(p * PW, PW)
        y_sends[s, p] = []
        for k in (2, 1, 3, 0):
            rows = pl.ds(pl.multiple_of(yy(k) * 64, 64), 64)
            part = c_own[s, rows, f] + c_recv[s, rows, f].astype(F32)
            if k:
                y_send[k - 1, s, :, f] = part.astype(BF)
                y_sends[s, p].append(
                    send(y_send.at[k - 1, s, :, f], y_recv.at[k - 1, s, :, f], at(y=yy(k)))
                )
            else:
                y_own[s, :, f] = part

    def din_l(s, p):
        for copy in y_sends[s, p]:
            copy.wait_recv()
        f = pl.ds(p * PW, PW)
        for which in (1 - l, l):
            rows = pl.ds(pl.multiple_of(which * 32, 32), 32)
            part = y_own[s, rows, f]
            for k in range(3):
                part = part + y_recv[k, s, rows, f].astype(F32)
            if which is l:
                l_own[s, :, f] = part
            else:
                l_send[s, :, f] = part.astype(BF)
                l_copies[s, p] = send(l_send.at[s, :, f], l_recv.at[s, :, f], other_l)

    def din_out_piece(s, p):
        l_copies[s, p].wait_recv()
        f = pl.ds(p * PW, PW)
        part = (l_own[s, :, f] + l_recv[s, :, f].astype(F32)).astype(BF)
        if s:
            o_send[:, f] = part
        for b in range(p * PW // BLOCK, (p + 1) * PW // BLOCK):
            there = pl.ds(pl.multiple_of((2 * b + h) * BLOCK, BLOCK), BLOCK)
            if s:
                o_copies.append(send(o_send.at[:, pl.ds(b * BLOCK, BLOCK)], o_buf.at[:, there], partner))
            else:
                o_buf[:, there] = part[:, (b * BLOCK - p * PW) : (b + 1) * BLOCK - p * PW]

    last = len(CHUNKS) - 1
    load_cot.wait()
    for copy in load_own:
        copy.wait()
    for k in range(last + 1):
        weights_and_pre(k)
        if k + EARLY <= last:
            send_noise(k + EARLY)
        if k:
            d_copies[k - 1].wait_recv()
            turn(1, k - 1)
            grads(k - 1)
        dpre(k)
    for p in range(PIECES):
        din_product(0, p)
    for p in range(PIECES):
        din_y(0, p)
    d_copies[last].wait_recv()
    turn(1, last)
    for p in range(PIECES):
        din_product(1, p)
    grads(last)
    for p in range(PIECES):
        din_y(1, p)
    for k in range(last):
        finish_sums(k)
    for p in range(PIECES):
        din_l(0, p)
    for p in range(PIECES):
        din_out_piece(0, p)
    finish_sums(last)
    for p in range(PIECES):
        din_l(1, p)
    for p in range(PIECES):
        din_out_piece(1, p)
    for copy in o_copies:
        copy.wait_recv()
    store = pltpu.make_async_copy(o_buf, din_out, lsem.at[2])
    store.start()
    store.wait()
    for copy in out_copies:
        copy.wait()
    t_near.wait_send()

    @pl.when(jnp.logical_not(stays))
    def _():
        t_far.wait_send()

    for copy in sent:
        copy.wait_send()


def communicate(tokens, noise, cotangent, mean, hess):
    vm = pltpu.VMEM
    units = (UNITS, BLOCK)
    scratch = [
        vm((2, BLOCK, WIDE), BF),
        vm((2, WIDE, BLOCK), BF),
        vm((UNITS, WIDE), BF),
        vm((UNITS, WIDE), BF),
        vm((2, UNITS, WIDE), BF),
        vm((2, UNITS, WIDE), BF),
        vm(units, BF),
        vm(units, F32),
        vm(units, F32),
        vm(units, F32),
        vm(units, BF),
        vm(units, BF),
        vm((2,) + units, BF),
        vm((2, 2, HALF, UNITS), BF),
        vm((3, 2) + units, BF),
        vm((3, 2) + units, BF),
        vm((2,) + units, F32),
        vm((2,) + units, F32),
        vm((2, HALF, WIDE), BF),
        vm((2, HALF, WIDE), BF),
        vm((2, HALF, WIDE), F32),
        vm((3, 2, 64, WIDE), BF),
        vm((3, 2, 64, WIDE), BF),
        vm((2, 64, WIDE), F32),
        vm((2, 32, WIDE), BF),
        vm((2, 32, WIDE), BF),
        vm((2, 32, WIDE), F32),
        vm((32, WIDE), BF),
        vm((32, 2 * WIDE), BF),
        pltpu.SemaphoreType.DMA((N_SEM,)),
        pltpu.SemaphoreType.DMA((N_SEM,)),
        pltpu.SemaphoreType.DMA((16,)),
    ]
    anywhere = pl.BlockSpec(memory_space=pl.ANY)
    return pl.pallas_call(
        kernel,
        out_shape=[
            jax.ShapeDtypeStruct((2,) + units, F32),
            jax.ShapeDtypeStruct((32, 2 * WIDE), BF),
        ],
        in_specs=[anywhere] * 5,
        out_specs=[anywhere] * 2,
        scratch_shapes=scratch,
        compiler_params=pltpu.CompilerParams(
            collective_id=1, has_side_effects=True, vmem_limit_bytes=62 << 20
        ),
        cost_estimate=pl.CostEstimate(flops=9 * 10**9, bytes_accessed=20 * 2**20, transcendentals=10**6),
    )(tokens, noise[0].T, cotangent.T, mean.T, hess.T)


def shards(tokens, noise, cotangent, mean, hess, momentum):
    n_rep = lax.axis_size("rep")
    sums, input_grad = communicate(tokens, noise, cotangent, mean, hess)
    grad_mean = sums[0].T / n_rep
    hess_mean = sums[1].T / n_rep
    new_momentum = 0.9 * momentum + 0.1 * grad_mean
    diff = hess - hess_mean
    new_hess = hess + 0.2 * (hess_mean - hess) + 0.5 * 0.04 * diff * diff / (hess + 0.001)
    new_mean = mean - 0.5 * (new_momentum + 0.001 * mean) / (new_hess + 0.001)
    return (new_mean, new_hess, new_momentum, input_grad)


def solution(mesh):
    in_specs = (
        P("rep", "tp"),
        P("rep", None, "tp"),
        P("rep", "tp"),
        P("rep", "tp"),
        P("rep", "tp"),
        P("rep", "tp"),
    )
    out_specs = (P("rep", "tp"), P("rep", "tp"), P("rep", "tp"), P(("rep", "tp"), None))
    return jax.shard_map(shards, mesh=mesh, in_specs=in_specs, out_specs=out_specs, check_vma=False)
```

time: 555 us -> 165 us (0.30)
  waiting for transfers between devices: 493 us -> 0 us
  Pallas kernels: 0 us -> 157 us
  matrix products: 29.6 us -> 0 us
  between operations: 14.2 us -> 0.66 us
  other arithmetic: 17.1 us -> 5.37 us
    reduce_scatter x3 -> x0, waiting for transfers between devices: 268 us -> none  [the longest x1 96.5 us: shards(): lax.psum_scatter(grad.astype(jnp.bfloat16), 'rep', scatter_dimension=0, t...]
    all_gather x3 -> x0, waiting for transfers between devices: 224 us -> none  [the longest x1 90.3 us: shards(): lax.all_gather(mean_low, 'rep', axis=0, tiled=True)]
    pallas_call x0 -> x1, Pallas kernels: none -> 157 us  [communicate(): pl.pallas_call(kernel, out_shape=[jax.ShapeDtypeStruct((2,) + units, F32)...]
    dot_general x3 -> x0, matrix products: 29.6 us -> none  [the longest x1 14.1 us: shards(): lax.dot_general(dpre, weight, (((1,), (1,)), ((), ())), preferred_element...]
    convert_element_type x4 -> x0, other arithmetic: 12.7 us -> none  [the longest x1 7.51 us: shards(): hest.astype(jnp.bfloat16)]
  transfers between devices with their start and end apart: 6 -> 0, of which waited for: 6 -> 0; matrix products, arithmetic and copies ran while one was open for 4% -> 0% of each run, Pallas kernels for 0% -> 0%
where the time goes in v1:
time: 165 us; the launch traced here: 164 us
  Pallas kernels  157 us (95%)
  other arithmetic  5.37 us (3%)
    pallas_call x1, Pallas kernels, communicate(): pl.pallas_call(kernel, out_shape=[jax.ShapeDtypeStruct((2,) + units, F32)...  157 us
    sub x1, other arithmetic, shards(): new_mean = mean - 0.5 * (new_momentum + 0.001 * mean) / (new_hess + 0.001)  5.37 us

profile of v1, /device:TPU:0, one launch (start us, length us, event | category | flops | bytes accessed | tf_op | source)
XLA Modules:
  0.0 164.0 jit_solution(7782557006072923417)
XLA Ops:
  0.6 0.0 copy-start
  0.6 157.3 %shard_map.93 = (f32[2,688,512]{2,1,0:T(8,128)}, bf16[32,4096]{1,0:T(8,128)(2,1)}) custom-call(bf16[512,256]{1,0:T(8,128)(2,1)} %tok_in.1, bf16[688,4096]{1,0:T(8,128)(2,1)} %bitcast.27, bf16[688,512]{1,0:T(8,128)(2,1)} %bitcast.28, f32[688,512]{1,0:T(8,128)} %bitcast.25, f32[688,512]{1,0:T(8,128)} %bitcast.26), custom_call_target="tpu_custom_call" | custom-call | flops 8999999488 | bytes 20971520 | tf_op jit(solution)/shard_map/pallas_call | solution.py:403
  157.9 0.0 copy-done
  158.0 0.0 copy-start.1
  158.0 5.4 %divide_subtract_fusion = (f32[512,688]{0,1:T(8,128)}, f32[512,688]{0,1:T(8,128)}, f32[512,688]{0,1:T(8,128)}) fusion(f32[512,688]{0,1:T(8,128)S(1)} %copy-done, f32[2,688,512]{2,1,0:T(8,128)} %get-tuple-element.6, f32[512,688]{0,1:T(8,128)} %param.11, f32[512,688]{0,1:T(8,128)} %param.10), kind=kLoop, calls=%fused_computation.8 | loop fusion | flops 6692864 | bytes 11272192 | tf_op jit(solution)/shard_map/sub | solution.py:427
  163.3 0.0 copy-done.1
  163.3 0.7 copy.11
Async XLA Ops:
  0.6 157.3 %copy-start = (f32[512,688]{0,1:T(8,128)S(1)}, f32[512,688]{0,1:T(8,128)}, u32[]{:S(2)}) copy-start(f32[512,688]{0,1:T(8,128)} %param.9) | copy-start | bytes 4227076
  158.0 5.4 %copy-start.1 = (bf16[32,4096]{1,0:T(8,128)(2,1)S(1)}, bf16[32,4096]{1,0:T(8,128)(2,1)}, u32[]{:S(2)}) copy-start(bf16[32,4096]{1,0:T(8,128)(2,1)} %get-tuple-element.18) | copy-start | bytes 786436

commit v2 on v0

v2 whole, which is shorter than its diff:
```python
import jax
import jax.numpy as jnp
from jax import lax
from jax.experimental import pallas as pl
from jax.experimental.pallas import tpu as pltpu
from jax.sharding import PartitionSpec as P

MESH = pl.DeviceIdType.MESH
BF, F32 = jnp.bfloat16, jnp.float32

NZ, NY = 4, 4
UNITS, BLOCK, WIDE = 688, 512, 2048
HALF = 256
CHUNKS = ((0, 128), (128, 128), (256, 128), (384, 128), (512, 128), (640, 48))
LAST = len(CHUNKS) - 1
AHEAD_FIRST, AHEAD = 12, 10
PIECES = 2
PW = WIDE // PIECES
PH = PW // 2
N_SEM = 192


def kernel(
    tok_in, noise_in, cot_in, mean_in, hess_in, mom_in,
    mean_out, hess_out, mom_out, din_out,
    tok, tokt, n_own, n_par, ms, wt, cot, mean_v, hess_v, mom_v,
    pre_own, p_send, p_recv, dp, dpt,
    up_send, up_recv, dn_send, dn_recv, up2_send, up2_recv, dn2_send, dn2_recv, g_keep, g_own,
    c_send, c_recv, c_own, yu_send, yu_recv, yd_send, yd_recv, yu2_send, yu2_recv, yd2_send, yd2_recv,
    f_send, f_recv, f_own, o_buf,
    ssem, rsem, lsem,
):
    rep, tp = lax.axis_index("rep"), lax.axis_index("tp")
    z, h = rep // 2, rep % 2
    y, l, c = tp // 4, (tp // 2) % 2, tp % 2

    def at(z=z, h=h, y=y, l=l, c=c):
        return (z * 2 + h, (y * 2 + l) * 2 + c)

    def zz(k):
        return lax.rem(z + k, NZ)

    def yy(k):
        return lax.rem(y + k, NY)

    partner, other_core, other_l = at(h=1 - h), at(c=1 - c), at(l=1 - l)
    z_up, z_dn, y_up, y_dn = at(z=zz(1)), at(z=zz(3)), at(y=yy(1)), at(y=yy(3))
    count = [2]
    sent = []

    def remote(src, dst, device, slot, rslot):
        return pltpu.make_async_remote_copy(
            src_ref=src, dst_ref=dst, send_sem=ssem.at[slot], recv_sem=rsem.at[rslot],
            device_id=device, device_id_type=MESH,
        )

    def send(src, dst, device):
        slot = count[0]
        count[0] += 1
        copy = remote(src, dst, device, slot, slot)
        copy.start()
        sent.append(copy)
        return copy

    peers = [other_l, partner, at(h=1 - h, l=1 - l), other_core, z_up, z_dn, y_up, y_dn]
    barrier = pltpu.get_barrier_semaphore()
    for peer in peers:
        pl.semaphore_signal(barrier, inc=1, device_id=peer, device_id_type=MESH)

    loads = []

    def load(src, dst):
        copy = pltpu.make_async_copy(src, dst, lsem.at[len(loads)])
        copy.start()
        loads.append(copy)
        return copy

    load_mean, load_hess = load(mean_in, mean_v), load(hess_in, hess_v)
    pl.semaphore_wait(barrier, len(peers))

    def tok_slot(s, at_y):
        return tok.at[s, :, pl.ds(pl.multiple_of(at_y * 512 + c * 256, 256), 256)]

    t_near = remote(tok_in, tok_slot(h, y), at(h=l, l=1 - l), 0, h)
    t_near.start()
    t_far = remote(tok_in, tok_slot(h, y), partner, 1, h)
    t_self = pltpu.make_async_copy(tok_in, tok_slot(h, y), rsem.at[h])
    stays = h == l

    @pl.when(stays)
    def _():
        t_self.start()

    @pl.when(jnp.logical_not(stays))
    def _():
        t_far.start()

    n_copies = []

    def send_noise(upto):
        for n in range(len(n_copies), min(upto, NZ * len(CHUNKS))):
            (first, rows), b = CHUNKS[n // NZ], n % NZ
            n_copies.append(
                send(
                    noise_in.at[pl.ds(first, rows), pl.ds(pl.multiple_of((2 * b + 1 - h) * BLOCK, BLOCK), BLOCK)],
                    n_par.at[pl.ds(first, rows), pl.ds(b * BLOCK, BLOCK)],
                    partner,
                )
            )

    send_noise(AHEAD_FIRST)
    load_own = [
        load(
            noise_in.at[:, pl.ds(pl.multiple_of((2 * b + h) * BLOCK, BLOCK), BLOCK)],
            n_own.at[:, pl.ds(b * BLOCK, BLOCK)],
        )
        for b in range(NZ)
    ]
    load_cot, load_mom = load(cot_in, cot), load(mom_in, mom_v)

    def z_block(k):
        return pl.ds(pl.multiple_of(zz(k) * BLOCK, BLOCK), BLOCK)

    own_z = z_block(0)
    s_up, s_dn, s_up2, s_dn2 = {}, {}, {}, {}

    def state(k):
        first, rows = CHUNKS[k]

        @pl.loop(0, rows // 16)
        def _(i):
            r = pl.ds(pl.multiple_of(first + i * 16, 16), 16)
            ms[0, r, own_z] = mean_v[r, :].astype(BF)
            ms[1, r, own_z] = lax.rsqrt(4.0 * (hess_v[r, :] + 0.001)).astype(BF)

        part = ms.at[:, pl.ds(first, rows), own_z]
        s_up[k], s_dn[k] = send(part, part, z_up), send(part, part, z_dn)

    def state_on(k):
        span = pl.ds(*CHUNKS[k])
        s_up[k].wait_recv()
        part = ms.at[0, span, z_block(3)]
        s_up2[k] = send(part, part, z_up)
        s_dn[k].wait_recv()
        part = ms.at[1, span, z_block(1)]
        s_dn2[k] = send(part, part, z_dn)

    load_mean.wait()
    load_hess.wait()
    state(0)
    state(1)

    t_up, t_dn, core = [], [], []
    for s in (h, 1 - h):
        slot = tok_slot(s, y)
        pltpu.make_async_copy(slot, slot, rsem.at[s]).wait()
        t_up.append(send(slot, slot, y_up))
        t_dn.append(send(slot, slot, y_dn))
        core.append(send(slot, slot, other_core))

    def token_on(copy, slot, device=None):
        copy.wait_recv()
        core.append(send(slot, slot, other_core))
        return None if device is None else send(slot, slot, device)

    state_on(0)
    state(2)
    t_up2 = token_on(t_up[0], tok_slot(h, yy(3)), y_up)
    token_on(t_dn[0], tok_slot(h, yy(1)))
    state_on(1)
    state(3)
    t_dn2 = token_on(t_dn[1], tok_slot(1 - h, yy(1)), y_dn)
    token_on(t_up[1], tok_slot(1 - h, yy(3)))
    state_on(2)
    state(4)
    token_on(t_up2, tok_slot(h, yy(2)))
    token_on(t_dn2, tok_slot(1 - h, yy(2)))
    for copy in core:
        copy.wait_recv()

    @pl.loop(0, 2 * WIDE // 256)
    def _(i):
        s, b = i // 8, i % 8
        f = pl.ds(pl.multiple_of(b * 256, 256), 256)
        tokt[s, f, :] = tok[s, :, f].T

    p_copies, d_copies = {}, {}

    def weights_and_pre(k):
        first, rows = CHUNKS[k]
        span = pl.ds(first, rows)
        for copy in (s_up2[k], s_dn2[k], *n_copies[NZ * k : NZ * k + NZ]):
            copy.wait_recv()

        @pl.loop(0, rows // 16)
        def _(i):
            r = pl.ds(pl.multiple_of(first + i * 16, 16), 16)
            for b in range(NZ):
                f = pl.ds(b * BLOCK, BLOCK)
                m, g = ms[0, r, f].astype(F32), ms[1, r, f].astype(F32)
                wt[0, r, f] = (m + g * n_own[r, f].astype(F32)).astype(BF)
                wt[1, r, f] = (m + g * n_par[r, f].astype(F32)).astype(BF)

        for half in range(2):
            t = pl.ds(half * HALF, HALF)
            p_send[span, t] = jnp.dot(wt[1, span, :], tokt[1 - h, :, t], preferred_element_type=F32).astype(BF)
        p_copies[k] = send(p_send.at[span], p_recv.at[span], partner)
        for half in range(2):
            t = pl.ds(half * HALF, HALF)
            pre_own[span, t] = jnp.dot(wt[0, span, :], tokt[h, :, t], preferred_element_type=F32)

    def turn(s, k):
        span = pl.ds(*CHUNKS[k])
        for t in range(16):
            if t % 4 == 0:
                turned = dp[s, span, t * 32 : t * 32 + 128].T
            dpt[s, t % 2, pl.ds(t // 2 * 32, 32), span] = turned[t % 4 * 32 : t % 4 * 32 + 32, :]

    def dpre(k):
        first, rows = CHUNKS[k]
        span = pl.ds(first, rows)
        p_copies[k].wait_recv()

        @pl.loop(0, rows // 16)
        def _(i):
            r = pl.ds(pl.multiple_of(first + i * 16, 16), 16)
            pre = pre_own[r, :] + p_recv[r, :].astype(F32)
            sig = 1.0 / (1.0 + jnp.exp(-pre))
            dp[0, r, :] = (cot[r, :].astype(F32) * sig * (1.0 + pre * (1.0 - sig))).astype(BF)

        d_copies[k] = send(dp.at[0, span], dp.at[1, span], partner)

    g_up, g_dn, g_up2, g_dn2 = {}, {}, {}, {}

    def grads(k):
        span = pl.ds(*CHUNKS[k])
        for step in (2, 1, 3, 0):
            for half in range(2):
                t = pl.ds(half * HALF, HALF)
                f = pl.ds(pl.multiple_of(zz(step) * BLOCK + half * HALF, HALF), HALF)
                one = jnp.dot(dp[0, span, :], tok[h, :, f], preferred_element_type=F32)
                two = jnp.dot(dp[1, span, :], tok[1 - h, :, f], preferred_element_type=F32)
                grad, hest = one + two, one * n_own[span, f].astype(F32) + two * n_par[span, f].astype(F32)
                if step == 2:
                    up_send[0, span, t] = grad.astype(BF)
                    dn_send[0, span, t] = hest.astype(BF)
                elif step == 1:
                    g_keep[0, span, t] = grad
                    up_send[1, span, t] = hest.astype(BF)
                elif step == 3:
                    dn_send[1, span, t] = grad.astype(BF)
                    g_keep[1, span, t] = hest
                else:
                    g_own[0, span, t] = grad
                    g_own[1, span, t] = hest
            if step == 1:
                g_up[k] = send(up_send.at[:, span], up_recv.at[:, span], z_up)
            elif step == 3:
                g_dn[k] = send(dn_send.at[:, span], dn_recv.at[:, span], z_dn)

    def grads_on(k):
        first, rows = CHUNKS[k]
        span = pl.ds(first, rows)
        g_up[k].wait_recv()
        up2_send[span, :] = (g_keep[0, span, :] + up_recv[0, span, :].astype(F32)).astype(BF)
        g_up2[k] = send(up2_send.at[span], up2_recv.at[span], z_up)
        g_dn[k].wait_recv()
        dn2_send[span, :] = (g_keep[1, span, :] + dn_recv[0, span, :].astype(F32)).astype(BF)
        g_dn2[k] = send(dn2_send.at[span], dn2_recv.at[span], z_dn)

    stores = []

    def store(src, dst):
        copy = pltpu.make_async_copy(src, dst, lsem.at[len(loads) + len(stores)])
        copy.start()
        stores.append(copy)

    def update(k):
        first, rows = CHUNKS[k]
        span = pl.ds(first, rows)
        g_up2[k].wait_recv()
        g_dn2[k].wait_recv()

        @pl.loop(0, rows // 16)
        def _(i):
            r = pl.ds(pl.multiple_of(first + i * 16, 16), 16)
            mean, hess = mean_v[r, :], hess_v[r, :]
            grad_mean = (g_own[0, r, :] + dn_recv[1, r, :].astype(F32) + up2_recv[r, :].astype(F32)) / 8.0
            hest = (g_own[1, r, :] + up_recv[1, r, :].astype(F32) + dn2_recv[r, :].astype(F32)) / 8.0
            hess_mean = hest / ms[1, r, own_z].astype(F32)
            new_momentum = 0.9 * mom_v[r, :] + 0.1 * grad_mean
            diff = hess - hess_mean
            new_hess = hess + 0.2 * (hess_mean - hess) + 0.5 * 0.04 * diff * diff / (hess + 0.001)
            mom_v[r, :] = new_momentum
            hess_v[r, :] = new_hess
            mean_v[r, :] = mean - 0.5 * (new_momentum + 0.001 * mean) / (new_hess + 0.001)

        store(mean_v.at[span], mean_out.at[span])
        store(hess_v.at[span], hess_out.at[span])
        store(mom_v.at[span], mom_out.at[span])

    c_copies, y_up1, y_dn1, y_up2, y_dn2, f_copies = {}, {}, {}, {}, {}, {}

    def din_product(s, p, keep):
        f = pl.ds(p * PW, PW)
        for q in range(PW // HALF):
            g = pl.ds(p * PW + q * HALF, HALF)
            part = jnp.dot(dpt[s, c if keep else 1 - c], wt[s, :, g], preferred_element_type=F32)
            if keep:
                c_own[s, :, g] = part
            else:
                c_send[s, :, g] = part.astype(BF)
        if not keep:
            c_copies[s, p] = send(c_send.at[s, :, f], c_recv.at[s, :, f], other_core)

    def din_products(s):
        for keep in (False, True):
            for p in range(PIECES):
                din_product(s, p, keep)

    def din_sum(s, p, k, second):
        rows = pl.ds(pl.multiple_of(yy(k) * 64, 64), 64)
        g = pl.ds(p * PW + second * PH, PH)
        return c_own[s, rows, g] + c_recv[s, rows, g].astype(F32)

    def din_y(s, p):
        c_copies[s, p].wait_recv()
        yu_send[s, p, 0] = din_sum(s, p, 2, 0).astype(BF)
        yu_send[s, p, 1] = din_sum(s, p, 1, 1).astype(BF)
        y_up1[s, p] = send(yu_send.at[s, p], yu_recv.at[s, p], y_up)
        yd_send[s, p, 0] = din_sum(s, p, 2, 1).astype(BF)
        yd_send[s, p, 1] = din_sum(s, p, 3, 0).astype(BF)
        y_dn1[s, p] = send(yd_send.at[s, p], yd_recv.at[s, p], y_dn)

    def din_y_on(s, p):
        y_up1[s, p].wait_recv()
        yu2_send[s, p] = (din_sum(s, p, 1, 0) + yu_recv[s, p, 0].astype(F32)).astype(BF)
        y_up2[s, p] = send(yu2_send.at[s, p], yu2_recv.at[s, p], y_up)
        y_dn1[s, p].wait_recv()
        yd2_send[s, p] = (din_sum(s, p, 3, 1) + yd_recv[s, p, 0].astype(F32)).astype(BF)
        y_dn2[s, p] = send(yd2_send.at[s, p], yd2_recv.at[s, p], y_dn)

    def din_last(s, p):
        y_up2[s, p].wait_recv()
        y_dn2[s, p].wait_recv()
        f = pl.ds(p * PW, PW)
        f_copies[s, p] = []
        for near in (False, True):
            which = l if near else 1 - l
            mine = pl.ds(pl.multiple_of(y * 64 + which * 32, 32), 32)
            rows = pl.ds(pl.multiple_of(which * 32, 32), 32)
            for second in range(2):
                g = pl.ds(p * PW + second * PH, PH)
                part = c_own[s, mine, g] + c_recv[s, mine, g].astype(F32)
                if second:
                    part = part + yu_recv[s, p, 1, rows, :].astype(F32) + yd2_recv[s, p, rows, :].astype(F32)
                else:
                    part = part + yd_recv[s, p, 1, rows, :].astype(F32) + yu2_recv[s, p, rows, :].astype(F32)
                if near and not s:
                    f_own[:, g] = part
                else:
                    f_send[s + near, :, g] = part.astype(BF)
            if s or not near:
                there = partner if near else at(h=1 - h, l=1 - l) if s else other_l
                f_copies[s, p].append(send(f_send.at[s + near, :, f], f_recv.at[s + near, :, f], there))

    def din_end(s, p):
        for copy in f_copies[s, p]:
            copy.wait_recv()
        for b in range(p * PW // BLOCK, (p + 1) * PW // BLOCK):
            f = pl.ds(b * BLOCK, BLOCK)
            there = pl.ds(pl.multiple_of((2 * b + (1 - h if s else h)) * BLOCK, BLOCK), BLOCK)
            if s:
                part = f_recv[1, :, f].astype(F32) + f_recv[2, :, f].astype(F32)
            else:
                part = f_own[:, f] + f_recv[0, :, f].astype(F32)
            o_buf[:, there] = part.astype(BF)

    load_cot.wait()
    for copy in load_own:
        copy.wait()
    for k in range(LAST + 1):
        weights_and_pre(k)
        if k == 0:
            send_noise(NZ + AHEAD)
            state_on(3)
            state(5)
        if k == 1:
            state_on(4)
        if k >= 1:
            dpre(k - 1)
            send_noise(NZ * (k + 1) + AHEAD)
            turn(0, k - 1)
        if k == 2:
            state_on(5)
        if k >= 2:
            d_copies[k - 2].wait_recv()
            grads(k - 2)
            turn(1, k - 2)
        if k >= 3:
            grads_on(k - 3)
        if k == 3:
            load_mom.wait()
        if k >= 4:
            update(k - 4)
    dpre(LAST)
    turn(0, LAST)
    din_products(0)
    d_copies[LAST - 1].wait_recv()
    grads(LAST - 1)
    turn(1, LAST - 1)
    din_y(0, 0)
    din_y(0, 1)
    grads_on(LAST - 2)
    d_copies[LAST].wait_recv()
    turn(1, LAST)
    din_products(1)
    grads(LAST)
    din_y_on(0, 0)
    din_y(1, 0)
    din_y_on(0, 1)
    din_y(1, 1)
    update(LAST - 3)
    grads_on(LAST - 1)
    din_y_on(1, 0)
    din_last(0, 0)
    din_last(0, 1)
    grads_on(LAST)
    update(LAST - 2)
    din_y_on(1, 1)
    din_last(1, 0)
    din_end(0, 0)
    din_end(0, 1)
    update(LAST - 1)
    din_last(1, 1)
    update(LAST)
    din_end(1, 0)
    din_end(1, 1)
    store(o_buf, din_out)
    for copy in stores:
        copy.wait()
    t_near.wait_send()

    @pl.when(jnp.logical_not(stays))
    def _():
        t_far.wait_send()

    for copy in sent:
        copy.wait_send()


def shards(tokens, noise, cotangent, mean, hess, momentum):
    vm = pltpu.VMEM
    units = (UNITS, BLOCK)
    piece = (2, PIECES, 64, PH)
    scratch = [
        vm((2, BLOCK, WIDE), BF),
        vm((2, WIDE, BLOCK), BF),
        vm((UNITS, WIDE), BF),
        vm((UNITS, WIDE), BF),
        vm((2, UNITS, WIDE), BF),
        vm((2, UNITS, WIDE), BF),
        vm(units, BF),
        vm(units, F32),
        vm(units, F32),
        vm(units, F32),
        vm(units, F32),
        vm(units, BF),
        vm(units, BF),
        vm((2,) + units, BF),
        vm((2, 2, HALF, UNITS), BF),
        *[vm((2,) + units, BF)] * 4,
        *[vm(units, BF)] * 4,
        vm((2,) + units, F32),
        vm((2,) + units, F32),
        vm((2, HALF, WIDE), BF),
        vm((2, HALF, WIDE), BF),
        vm((2, HALF, WIDE), F32),
        *[vm((2, PIECES, 2, 64, PH), BF)] * 4,
        *[vm(piece, BF)] * 4,
        vm((3, 32, WIDE), BF),
        vm((3, 32, WIDE), BF),
        vm((32, WIDE), F32),
        vm((32, 2 * WIDE), BF),
        pltpu.SemaphoreType.DMA((N_SEM,)),
        pltpu.SemaphoreType.DMA((N_SEM,)),
        pltpu.SemaphoreType.DMA((32,)),
    ]
    anywhere = pl.BlockSpec(memory_space=pl.ANY)
    new_mean, new_hess, new_momentum, input_grad = pl.pallas_call(
        kernel,
        out_shape=[jax.ShapeDtypeStruct(units, F32)] * 3 + [jax.ShapeDtypeStruct((32, 2 * WIDE), BF)],
        in_specs=[anywhere] * 6,
        out_specs=[anywhere] * 4,
        scratch_shapes=scratch,
        compiler_params=pltpu.CompilerParams(
            collective_id=1, has_side_effects=True, vmem_limit_bytes=63 << 20
        ),
        cost_estimate=pl.CostEstimate(flops=9 * 10**9, bytes_accessed=20 * 2**20, transcendentals=10**6),
    )(tokens, noise[0].T, cotangent.T, mean.T, hess.T, momentum.T)
    return (new_mean.T, new_hess.T, new_momentum.T, input_grad)


def solution(mesh):
    in_specs = (
        P("rep", "tp"),
        P("rep", None, "tp"),
        P("rep", "tp"),
        P("rep", "tp"),
        P("rep", "tp"),
        P("rep", "tp"),
    )
    out_specs = (P("rep", "tp"), P("rep", "tp"), P("rep", "tp"), P(("rep", "tp"), None))
    return jax.shard_map(shards, mesh=mesh, in_specs=in_specs, out_specs=out_specs, check_vma=False)
```

time: 555 us -> 145 us (0.26)
  waiting for transfers between devices: 493 us -> 0 us
  Pallas kernels: 0 us -> 138 us
  matrix products: 29.6 us -> 0 us
  other arithmetic: 17.1 us -> 0 us
  between operations: 14.2 us -> 0.65 us
  local copies, waits for them, and re-layouts: 0.02 us -> 6.31 us
    reduce_scatter x3 -> x0, waiting for transfers between devices: 268 us -> none  [the longest x1 96.5 us: shards(): lax.psum_scatter(grad.astype(jnp.bfloat16), 'rep', scatter_dimension=0, t...]
    all_gather x3 -> x0, waiting for transfers between devices: 224 us -> none  [the longest x1 90.3 us: shards(): lax.all_gather(mean_low, 'rep', axis=0, tiled=True)]
    pallas_call x0 -> x1, Pallas kernels: none -> 138 us  [shards(): pl.pallas_call(kernel, out_shape=[jax.ShapeDtypeStruct(units, F32)] * 3 +...]
    dot_general x3 -> x0, matrix products: 29.6 us -> none  [the longest x1 14.1 us: shards(): lax.dot_general(dpre, weight, (((1,), (1,)), ((), ())), preferred_element...]
    convert_element_type x4 -> x0, other arithmetic: 12.7 us -> none  [the longest x1 7.51 us: shards(): hest.astype(jnp.bfloat16)]
    unnamed x10, local copies, waits for them, and re-layouts: 0.02 us -> 6.31 us
  transfers between devices with their start and end apart: 6 -> 0, of which waited for: 6 -> 0; matrix products, arithmetic and copies ran while one was open for 4% -> 0% of each run, Pallas kernels for 0% -> 0%
where the time goes in v2:
time: 145 us
  Pallas kernels  138 us (95%)
  local copies, waits for them, and re-layouts  6.31 us (4%)
    pallas_call x1, Pallas kernels, shards(): pl.pallas_call(kernel, out_shape=[jax.ShapeDtypeStruct(units, F32)] * 3 +...  138 us
    unnamed x10, local copies, waits for them, and re-layouts  6.31 us

profile of v2, /device:TPU:0, one launch (start us, length us, event | category | flops | bytes accessed | tf_op | source)
XLA Modules:
  0.0 144.7 jit_solution(14676001604503536669)
XLA Ops:
  0.6 137.7 %shard_map.93 = (f32[688,512]{1,0:T(8,128)}, f32[688,512]{1,0:T(8,128)}, f32[688,512]{1,0:T(8,128)}, bf16[32,4096]{1,0:T(8,128)(2,1)}) custom-call(bf16[512,256]{1,0:T(8,128)(2,1)} %tok_in.1, bf16[688,4096]{1,0:T(8,128)(2,1)} %bitcast.13, bf16[688,512]{1,0:T(8,128)(2,1)} %bitcast.17, f32[688,512]{1,0:T(8,128)} %bitcast.14, f32[688,512]{1,0:T(8,128)} %bitcast.15, ...), custom_call_target="tpu_custom_call" | custom-call | flops 8999999488 | bytes 20971520 | tf_op jit(solution)/shard_map/pallas_call | solution.py:490
  138.4 0.0 copy-start.1
  138.4 2.6 %copy.14 = f32[512,688]{0,1:T(8,128)} copy(f32[512,688]{0,1:T(8,128)} %bitcast.12) | data formatting | bytes 2818048
  141.0 0.0 copy-done.1
  141.0 0.0 copy-start
  141.0 1.1 copy.15
  142.1 0.8 copy-done
  142.9 0.0 copy-start.2
  142.9 1.1 copy.16
  144.0 0.0 copy-done.2
  144.0 0.7 copy.17
Async XLA Ops:
  138.4 2.7 %copy-start.1 = (f32[688,512]{1,0:T(8,128)S(1)}, f32[688,512]{1,0:T(8,128)}, u32[]{:S(2)}) copy-start(f32[688,512]{1,0:T(8,128)} %get-tuple-element.9) | copy-start | bytes 4227076
  141.0 1.9 %copy-start = (f32[688,512]{1,0:T(8,128)S(1)}, f32[688,512]{1,0:T(8,128)}, u32[]{:S(2)}) copy-start(f32[688,512]{1,0:T(8,128)} %get-tuple-element.10) | copy-start | bytes 4227076
  142.9 1.1 copy-start.2

commit v3 on v2

--- a/solution.py
+++ b/solution.py
@@ -13,11 +13,29 @@
 HALF = 256
 CHUNKS = ((0, 128), (128, 128), (256, 128), (384, 128), (512, 128), (640, 48))
 LAST = len(CHUNKS) - 1
-AHEAD_FIRST, AHEAD = 12, 10
 PIECES = 2
 PW = WIDE // PIECES
 PH = PW // 2
+X_FIRST = ((0, 1),)
 N_SEM = 192
+ORDER = (
+    ("noise", 10), ("state", 0), ("state", 1), ("state", 2), ("state_up", 0), ("state_dn", 0), ("token", 0),
+    ("token", 1), ("state_up", 1), ("state_dn", 1), ("token_up", 0), ("token_dn", 0), ("state", 3), ("state_up", 2),
+    ("state_dn", 2), ("token_up", 1), ("token_dn", 1), ("state", 4), ("token_up", 2), ("noise", 11), ("token_dn", 2),
+    ("state_up", 3), ("state_dn", 3), ("noise", 12), ("tokens", 0), ("A", 0), ("A", 1), ("state", 5), ("state_up", 4),
+    ("state_dn", 4), ("noise", 14), ("A", 2), ("state_dn", 5), ("state_up", 5), ("B", 0), ("B", 1), ("noise", 16),
+    ("B", 2), ("turn", 0), ("C", 0), ("noise", 17), ("turn", 1), ("C", 1), ("noise", 19), ("on_up", 0), ("A", 3),
+    ("on_dn", 0), ("turn", 2), ("C", 2), ("noise", 20), ("on_up", 1), ("on_dn", 1), ("noise", 21), ("update", 0),
+    ("noise", 24), ("on_up", 2), ("B", 3), ("on_dn", 2), ("A", 4), ("update", 1), ("update", 2), ("A", 5),
+    ("turn", 3), ("C", 3), ("B", 4), ("B", 5), ("prod_send", 0, 0), ("prod_send", 0, 1), ("prod_own", 0, 0),
+    ("prod_own", 0, 1), ("y", 0, 0), ("x_first", 0, 1), ("turn", 4), ("C", 4), ("turn", 5), ("prod_send", 1, 0),
+    ("prod_send", 1, 1), ("C", 5), ("on_dn", 3), ("prod_own", 1, 0), ("y_up", 0, 0), ("y_dn", 0, 0),
+    ("prod_own", 1, 1), ("on_up", 3), ("y", 1, 0), ("y", 1, 1), ("y", 0, 1), ("last", 0, 0), ("on_up", 4),
+    ("on_dn", 4), ("y_up", 1, 0), ("y_dn", 1, 0), ("on_up", 5), ("on_dn", 5), ("end", 0, 0), ("y_up", 1, 1),
+    ("y_dn", 1, 1), ("update", 3), ("y_up", 0, 1), ("y_dn", 0, 1), ("last", 1, 0), ("update", 4), ("last", 1, 1),
+    ("update", 5), ("last_own", 0, 1), ("end", 1, 0), ("end", 1, 1),
+)
+PARTS = 2
 
 
 def kernel(
@@ -27,7 +45,7 @@
     pre_own, p_send, p_recv, dp, dpt,
     up_send, up_recv, dn_send, dn_recv, up2_send, up2_recv, dn2_send, dn2_recv, g_keep, g_own,
     c_send, c_recv, c_own, yu_send, yu_recv, yd_send, yd_recv, yu2_send, yu2_recv, yd2_send, yd2_recv,
-    f_send, f_recv, f_own, o_buf,
+    x_send, x_recv, f_send, f_recv, f_own, o_buf,
     ssem, rsem, lsem,
 ):
     rep, tp = lax.axis_index("rep"), lax.axis_index("tp")
@@ -54,11 +72,12 @@
             device_id=device, device_id_type=MESH,
         )
 
-    def send(src, dst, device):
+    def send(src, dst, device, start=True):
         slot = count[0]
         count[0] += 1
         copy = remote(src, dst, device, slot, slot)
-        copy.start()
+        if start:
+            copy.start()
         sent.append(copy)
         return copy
 
@@ -97,7 +116,7 @@
 
     n_copies = []
 
-    def send_noise(upto):
+    def send_noise(upto, start=True):
         for n in range(len(n_copies), min(upto, NZ * len(CHUNKS))):
             (first, rows), b = CHUNKS[n // NZ], n % NZ
             n_copies.append(
@@ -105,10 +124,11 @@
                     noise_in.at[pl.ds(first, rows), pl.ds(pl.multiple_of((2 * b + 1 - h) * BLOCK, BLOCK), BLOCK)],
                     n_par.at[pl.ds(first, rows), pl.ds(b * BLOCK, BLOCK)],
                     partner,
+                    start,
                 )
             )
 
-    send_noise(AHEAD_FIRST)
+    send_noise(ORDER[0][1])
     load_own = [
         load(
             noise_in.at[:, pl.ds(pl.multiple_of((2 * b + h) * BLOCK, BLOCK), BLOCK)],
@@ -136,53 +156,56 @@
         part = ms.at[:, pl.ds(first, rows), own_z]
         s_up[k], s_dn[k] = send(part, part, z_up), send(part, part, z_dn)
 
-    def state_on(k):
-        span = pl.ds(*CHUNKS[k])
+    def state_up(k):
         s_up[k].wait_recv()
-        part = ms.at[0, span, z_block(3)]
+        part = ms.at[0, pl.ds(*CHUNKS[k]), z_block(3)]
         s_up2[k] = send(part, part, z_up)
+
+    def state_dn(k):
         s_dn[k].wait_recv()
-        part = ms.at[1, span, z_block(1)]
+        part = ms.at[1, pl.ds(*CHUNKS[k]), z_block(1)]
         s_dn2[k] = send(part, part, z_dn)
 
     load_mean.wait()
     load_hess.wait()
-    state(0)
-    state(1)
-
-    t_up, t_dn, core = [], [], []
-    for s in (h, 1 - h):
+
+    t_up, t_dn, core = {}, {}, []
+
+    def token(k):
+        s = 1 - h if k else h
         slot = tok_slot(s, y)
         pltpu.make_async_copy(slot, slot, rsem.at[s]).wait()
-        t_up.append(send(slot, slot, y_up))
-        t_dn.append(send(slot, slot, y_dn))
+        t_up[k] = send(slot, slot, y_up)
+        t_dn[k] = send(slot, slot, y_dn)
         core.append(send(slot, slot, other_core))
 
-    def token_on(copy, slot, device=None):
-        copy.wait_recv()
+    def token_up(k):
+        t_up[k].wait_recv()
+        slot = tok_slot(1 - h if k == 1 else h, yy(2 if k == 2 else 3))
         core.append(send(slot, slot, other_core))
-        return None if device is None else send(slot, slot, device)
-
-    state_on(0)
-    state(2)
-    t_up2 = token_on(t_up[0], tok_slot(h, yy(3)), y_up)
-    token_on(t_dn[0], tok_slot(h, yy(1)))
-    state_on(1)
-    state(3)
-    t_dn2 = token_on(t_dn[1], tok_slot(1 - h, yy(1)), y_dn)
-    token_on(t_up[1], tok_slot(1 - h, yy(3)))
-    state_on(2)
-    state(4)
-    token_on(t_up2, tok_slot(h, yy(2)))
-    token_on(t_dn2, tok_slot(1 - h, yy(2)))
-    for copy in core:
-        copy.wait_recv()
-
-    @pl.loop(0, 2 * WIDE // 256)
-    def _(i):
-        s, b = i // 8, i % 8
-        f = pl.ds(pl.multiple_of(b * 256, 256), 256)
-        tokt[s, f, :] = tok[s, :, f].T
+        if k == 0:
+            t_up[2] = send(slot, slot, y_up)
+
+    def token_dn(k):
+        t_dn[k].wait_recv()
+        slot = tok_slot(h if k == 0 else 1 - h, yy(2 if k == 2 else 1))
+        core.append(send(slot, slot, other_core))
+        if k == 1:
+            t_dn[2] = send(slot, slot, y_dn)
+
+    def tokens(_):
+        for copy in core:
+            copy.wait_recv()
+
+        @pl.loop(0, 2 * WIDE // 256)
+        def _(i):
+            s, b = i // 8, i % 8
+            f = pl.ds(pl.multiple_of(b * 256, 256), 256)
+            tokt[s, f, :] = tok[s, :, f].T
+
+        load_cot.wait()
+        for copy in load_own:
+            copy.wait()
 
     p_copies, d_copies = {}, {}
 
@@ -229,10 +252,23 @@
             dp[0, r, :] = (cot[r, :].astype(F32) * sig * (1.0 + pre * (1.0 - sig))).astype(BF)
 
         d_copies[k] = send(dp.at[0, span], dp.at[1, span], partner)
+        turn(0, k)
 
     g_up, g_dn, g_up2, g_dn2 = {}, {}, {}, {}
 
+    came = set()
+
+    def dpre_here(k):
+        if k not in came:
+            d_copies[k].wait_recv()
+            came.add(k)
+
+    def turn_other(k):
+        dpre_here(k)
+        turn(1, k)
+
     def grads(k):
+        dpre_here(k)
         span = pl.ds(*CHUNKS[k])
         for step in (2, 1, 3, 0):
             for half in range(2):
@@ -258,12 +294,14 @@
             elif step == 3:
                 g_dn[k] = send(dn_send.at[:, span], dn_recv.at[:, span], z_dn)
 
-    def grads_on(k):
-        first, rows = CHUNKS[k]
-        span = pl.ds(first, rows)
+    def on_up(k):
+        span = pl.ds(*CHUNKS[k])
         g_up[k].wait_recv()
         up2_send[span, :] = (g_keep[0, span, :] + up_recv[0, span, :].astype(F32)).astype(BF)
         g_up2[k] = send(up2_send.at[span], up2_recv.at[span], z_up)
+
+    def on_dn(k):
+        span = pl.ds(*CHUNKS[k])
         g_dn[k].wait_recv()
         dn2_send[span, :] = (g_keep[1, span, :] + dn_recv[0, span, :].astype(F32)).astype(BF)
         g_dn2[k] = send(dn2_send.at[span], dn2_recv.at[span], z_dn)
@@ -277,6 +315,8 @@
 
     def update(k):
         first, rows = CHUNKS[k]
+        if k == 0:
+            load_mom.wait()
         span = pl.ds(first, rows)
         g_up2[k].wait_recv()
         g_dn2[k].wait_recv()
@@ -313,32 +353,66 @@
         if not keep:
             c_copies[s, p] = send(c_send.at[s, :, f], c_recv.at[s, :, f], other_core)
 
-    def din_products(s):
-        for keep in (False, True):
-            for p in range(PIECES):
-                din_product(s, p, keep)
+    x_copies = {}
+
+    def din_x_first(s, p):
+        c_copies[s, p].wait_recv()
+        f = pl.ds(p * PW, PW)
+        for k in range(NY):
+            rows = pl.ds(pl.multiple_of(k * 64 + (1 - l) * 32, 32), 32)
+            x_send[pl.ds(k * 32, 32), :] = (c_own[s, rows, f] + c_recv[s, rows, f].astype(F32)).astype(BF)
+        x_copies[s, p] = send(x_send, x_recv, other_l)
+
+    def depth(s, p):
+        return 32 if (s, p) in X_FIRST else 64
 
     def din_sum(s, p, k, second):
+        g = pl.ds(p * PW + second * PH, PH)
+        if (s, p) in X_FIRST:
+            rows = pl.ds(pl.multiple_of(yy(k) * 64 + l * 32, 32), 32)
+            there = pl.ds(pl.multiple_of(yy(k) * 32, 32), 32)
+            return c_own[s, rows, g] + (
+                c_recv[s, rows, g].astype(F32) + x_recv[there, pl.ds(second * PH, PH)].astype(F32)
+            )
         rows = pl.ds(pl.multiple_of(yy(k) * 64, 64), 64)
-        g = pl.ds(p * PW + second * PH, PH)
         return c_own[s, rows, g] + c_recv[s, rows, g].astype(F32)
 
     def din_y(s, p):
-        c_copies[s, p].wait_recv()
-        yu_send[s, p, 0] = din_sum(s, p, 2, 0).astype(BF)
-        yu_send[s, p, 1] = din_sum(s, p, 1, 1).astype(BF)
-        y_up1[s, p] = send(yu_send.at[s, p], yu_recv.at[s, p], y_up)
-        yd_send[s, p, 0] = din_sum(s, p, 2, 1).astype(BF)
-        yd_send[s, p, 1] = din_sum(s, p, 3, 0).astype(BF)
-        y_dn1[s, p] = send(yd_send.at[s, p], yd_recv.at[s, p], y_dn)
-
-    def din_y_on(s, p):
+        (x_copies if (s, p) in X_FIRST else c_copies)[s, p].wait_recv()
+        d = pl.ds(0, depth(s, p))
+        yu_send[s, p, 0, d] = din_sum(s, p, 2, 0).astype(BF)
+        yu_send[s, p, 1, d] = din_sum(s, p, 1, 1).astype(BF)
+        y_up1[s, p] = send(yu_send.at[s, p, :, d], yu_recv.at[s, p, :, d], y_up)
+        yd_send[s, p, 0, d] = din_sum(s, p, 2, 1).astype(BF)
+        yd_send[s, p, 1, d] = din_sum(s, p, 3, 0).astype(BF)
+        y_dn1[s, p] = send(yd_send.at[s, p, :, d], yd_recv.at[s, p, :, d], y_dn)
+
+    def din_y_up(s, p):
+        d = pl.ds(0, depth(s, p))
         y_up1[s, p].wait_recv()
-        yu2_send[s, p] = (din_sum(s, p, 1, 0) + yu_recv[s, p, 0].astype(F32)).astype(BF)
-        y_up2[s, p] = send(yu2_send.at[s, p], yu2_recv.at[s, p], y_up)
+        yu2_send[s, p, d] = (din_sum(s, p, 1, 0) + yu_recv[s, p, 0, d].astype(F32)).astype(BF)
+        y_up2[s, p] = send(yu2_send.at[s, p, d], yu2_recv.at[s, p, d], y_up)
+
+    def din_y_dn(s, p):
+        d = pl.ds(0, depth(s, p))
         y_dn1[s, p].wait_recv()
-        yd2_send[s, p] = (din_sum(s, p, 3, 1) + yd_recv[s, p, 0].astype(F32)).astype(BF)
-        y_dn2[s, p] = send(yd2_send.at[s, p], yd2_recv.at[s, p], y_dn)
+        yd2_send[s, p, d] = (din_sum(s, p, 3, 1) + yd_recv[s, p, 0, d].astype(F32)).astype(BF)
+        y_dn2[s, p] = send(yd2_send.at[s, p, d], yd2_recv.at[s, p, d], y_dn)
+
+    def din_last_own(s, p):
+        y_up2[s, p].wait_recv()
+        y_dn2[s, p].wait_recv()
+        d = pl.ds(0, depth(s, p))
+        for second in range(2):
+            part = din_sum(s, p, 0, second)
+            if second:
+                part = part + yu_recv[s, p, 1, d].astype(F32) + yd2_recv[s, p, d].astype(F32)
+            else:
+                part = part + yd_recv[s, p, 1, d].astype(F32) + yu2_recv[s, p, d].astype(F32)
+            for b in range(PH // BLOCK):
+                block = (p * PW + second * PH) // BLOCK + b
+                there = pl.ds(pl.multiple_of((2 * block + h) * BLOCK, BLOCK), BLOCK)
+                o_buf[:, there] = part[:, b * BLOCK : (b + 1) * BLOCK].astype(BF)
 
     def din_last(s, p):
         y_up2[s, p].wait_recv()
@@ -376,66 +450,17 @@
                 part = f_own[:, f] + f_recv[0, :, f].astype(F32)
             o_buf[:, there] = part.astype(BF)
 
-    load_cot.wait()
-    for copy in load_own:
-        copy.wait()
-    for k in range(LAST + 1):
-        weights_and_pre(k)
-        if k == 0:
-            send_noise(NZ + AHEAD)
-            state_on(3)
-            state(5)
-        if k == 1:
-            state_on(4)
-        if k >= 1:
-            dpre(k - 1)
-            send_noise(NZ * (k + 1) + AHEAD)
-            turn(0, k - 1)
-        if k == 2:
-            state_on(5)
-        if k >= 2:
-            d_copies[k - 2].wait_recv()
-            grads(k - 2)
-            turn(1, k - 2)
-        if k >= 3:
-            grads_on(k - 3)
-        if k == 3:
-            load_mom.wait()
-        if k >= 4:
-            update(k - 4)
-    dpre(LAST)
-    turn(0, LAST)
-    din_products(0)
-    d_copies[LAST - 1].wait_recv()
-    grads(LAST - 1)
-    turn(1, LAST - 1)
-    din_y(0, 0)
-    din_y(0, 1)
-    grads_on(LAST - 2)
-    d_copies[LAST].wait_recv()
-    turn(1, LAST)
-    din_products(1)
-    grads(LAST)
-    din_y_on(0, 0)
-    din_y(1, 0)
-    din_y_on(0, 1)
-    din_y(1, 1)
-    update(LAST - 3)
-    grads_on(LAST - 1)
-    din_y_on(1, 0)
-    din_last(0, 0)
-    din_last(0, 1)
-    grads_on(LAST)
-    update(LAST - 2)
-    din_y_on(1, 1)
-    din_last(1, 0)
-    din_end(0, 0)
-    din_end(0, 1)
-    update(LAST - 1)
-    din_last(1, 1)
-    update(LAST)
-    din_end(1, 0)
-    din_end(1, 1)
+    steps = {
+        "noise": send_noise, "state": state, "state_up": state_up, "state_dn": state_dn,
+        "token": token, "token_up": token_up, "token_dn": token_dn, "tokens": tokens,
+        "A": weights_and_pre, "B": dpre, "turn": turn_other, "C": grads,
+        "on_up": on_up, "on_dn": on_dn, "update": update,
+        "prod_send": lambda s, p: din_product(s, p, False), "prod_own": lambda s, p: din_product(s, p, True),
+        "x_first": din_x_first, "y": din_y, "y_up": din_y_up, "y_dn": din_y_dn,
+        "last": din_last, "last_own": din_last_own, "end": din_end,
+    }
+    for name, *where in ORDER:
+        steps[name](*where)
     store(o_buf, din_out)
     for copy in stores:
         copy.wait()
@@ -447,6 +472,12 @@
 
     for copy in sent:
         copy.wait_send()
+
+
+def settle(*refs):
+    n = len(refs) // 2
+    for src, dst in zip(refs[:n], refs[n:]):
+        dst[...] = src[...]
 
 
 def shards(tokens, noise, cotangent, mean, hess, momentum):
@@ -478,6 +509,8 @@
         vm((2, HALF, WIDE), F32),
         *[vm((2, PIECES, 2, 64, PH), BF)] * 4,
         *[vm(piece, BF)] * 4,
+        vm((128, PW), BF),
+        vm((128, PW), BF),
         vm((3, 32, WIDE), BF),
         vm((3, 32, WIDE), BF),
         vm((32, WIDE), F32),
@@ -487,9 +520,10 @@
         pltpu.SemaphoreType.DMA((32,)),
     ]
     anywhere = pl.BlockSpec(memory_space=pl.ANY)
-    new_mean, new_hess, new_momentum, input_grad = pl.pallas_call(
+    outs = [jax.ShapeDtypeStruct(units, F32)] * 3 + [jax.ShapeDtypeStruct((32, 2 * WIDE), BF)]
+    results = pl.pallas_call(
         kernel,
-        out_shape=[jax.ShapeDtypeStruct(units, F32)] * 3 + [jax.ShapeDtypeStruct((32, 2 * WIDE), BF)],
+        out_shape=outs,
         in_specs=[anywhere] * 6,
         out_specs=[anywhere] * 4,
         scratch_shapes=scratch,
@@ -498,6 +532,16 @@
         ),
         cost_estimate=pl.CostEstimate(flops=9 * 10**9, bytes_accessed=20 * 2**20, transcendentals=10**6),
     )(tokens, noise[0].T, cotangent.T, mean.T, hess.T, momentum.T)
+    blocks = [pl.BlockSpec((o.shape[0] // PARTS, o.shape[1]), lambda i: (i, 0)) for o in outs]
+    new_mean, new_hess, new_momentum, input_grad = pl.pallas_call(
+        settle,
+        grid=(PARTS,),
+        out_shape=outs,
+        in_specs=blocks,
+        out_specs=blocks,
+        compiler_params=pltpu.CompilerParams(vmem_limit_bytes=63 << 20),
+        cost_estimate=pl.CostEstimate(flops=0, bytes_accessed=9 * 2**20, transcendentals=0),
+    )(*results)
     return (new_mean.T, new_hess.T, new_momentum.T, input_grad)
 
 

time: 145 us -> 138 us (0.952)
  local copies, waits for them, and re-layouts: 6.31 us -> 0 us
    unnamed x10 -> x0, local copies, waits for them, and re-layouts: 6.31 us -> none
    pallas_call x1 -> x2, Pallas kernels: 138 us -> 137 us  [the longest x1 133 us: shards(): pl.pallas_call(kernel, out_shape=outs, in_specs=[anywhere] * 6, out_specs...]
where the time goes in v3:
time: 138 us; the launch traced here: 137 us
  Pallas kernels  137 us (99%)
    pallas_call x1, Pallas kernels, shards(): pl.pallas_call(kernel, out_shape=outs, in_specs=[anywhere] * 6, out_specs...  133 us
    pallas_call x1, Pallas kernels, shards(): pl.pallas_call(settle, grid=(PARTS,), out_shape=outs, in_specs=blocks, ou...  3.8 us

profile of v3, /device:TPU:0, one launch (start us, length us, event | category | flops | bytes accessed | tf_op | source)
XLA Modules:
  0.0 137.4 jit_solution(11486215404574468483)
XLA Ops:
  0.6 133.0 %shard_map.93 = (f32[688,512]{1,0:T(8,128)}, f32[688,512]{1,0:T(8,128)}, f32[688,512]{1,0:T(8,128)}, bf16[32,4096]{1,0:T(8,128)(2,1)}) custom-call(bf16[512,256]{1,0:T(8,128)(2,1)} %tok_in.1, bf16[688,4096]{1,0:T(8,128)(2,1)} %bitcast.10, bf16[688,512]{1,0:T(8,128)(2,1)} %bitcast.17, f32[688,512]{1,0:T(8,128)} %bitcast.11, f32[688,512]{1,0:T(8,128)} %bitcast.12, ...), custom_call_target="tpu_custom_call" | custom-call | flops 8999999488 | bytes 20971520 | tf_op jit(solution)/shard_map/pallas_call | solution.py:524
  133.6 3.8 %shard_map.94 = (f32[688,512]{1,0:T(8,128)}, f32[688,512]{1,0:T(8,128)}, f32[688,512]{1,0:T(8,128)}, bf16[32,4096]{1,0:T(8,128)(2,1)}) custom-call(f32[688,512]{1,0:T(8,128)} %get-tuple-element.12.refs_0_, f32[688,512]{1,0:T(8,128)} %get-tuple-element.13.refs_1_, f32[688,512]{1,0:T(8,128)} %get-tuple-element.14.refs_2_, ...), custom_call_target="tpu_custom_call" | custom-call | bytes 9437184 | tf_op jit(solution)/shard_map/pallas_call | solution.py:536

commit v4 on v3

--- a/solution.py
+++ b/solution.py
@@ -13,27 +13,32 @@
 HALF = 256
 CHUNKS = ((0, 128), (128, 128), (256, 128), (384, 128), (512, 128), (640, 48))
 LAST = len(CHUNKS) - 1
-PIECES = 2
+PIECES = 4
 PW = WIDE // PIECES
 PH = PW // 2
-X_FIRST = ((0, 1),)
+X_FIRST = ((0, 3),)
 N_SEM = 192
 ORDER = (
-    ("noise", 10), ("state", 0), ("state", 1), ("state", 2), ("state_up", 0), ("state_dn", 0), ("token", 0),
-    ("token", 1), ("state_up", 1), ("state_dn", 1), ("token_up", 0), ("token_dn", 0), ("state", 3), ("state_up", 2),
-    ("state_dn", 2), ("token_up", 1), ("token_dn", 1), ("state", 4), ("token_up", 2), ("noise", 11), ("token_dn", 2),
-    ("state_up", 3), ("state_dn", 3), ("noise", 12), ("tokens", 0), ("A", 0), ("A", 1), ("state", 5), ("state_up", 4),
-    ("state_dn", 4), ("noise", 14), ("A", 2), ("state_dn", 5), ("state_up", 5), ("B", 0), ("B", 1), ("noise", 16),
-    ("B", 2), ("turn", 0), ("C", 0), ("noise", 17), ("turn", 1), ("C", 1), ("noise", 19), ("on_up", 0), ("A", 3),
-    ("on_dn", 0), ("turn", 2), ("C", 2), ("noise", 20), ("on_up", 1), ("on_dn", 1), ("noise", 21), ("update", 0),
-    ("noise", 24), ("on_up", 2), ("B", 3), ("on_dn", 2), ("A", 4), ("update", 1), ("update", 2), ("A", 5),
-    ("turn", 3), ("C", 3), ("B", 4), ("B", 5), ("prod_send", 0, 0), ("prod_send", 0, 1), ("prod_own", 0, 0),
-    ("prod_own", 0, 1), ("y", 0, 0), ("x_first", 0, 1), ("turn", 4), ("C", 4), ("turn", 5), ("prod_send", 1, 0),
-    ("prod_send", 1, 1), ("C", 5), ("on_dn", 3), ("prod_own", 1, 0), ("y_up", 0, 0), ("y_dn", 0, 0),
-    ("prod_own", 1, 1), ("on_up", 3), ("y", 1, 0), ("y", 1, 1), ("y", 0, 1), ("last", 0, 0), ("on_up", 4),
-    ("on_dn", 4), ("y_up", 1, 0), ("y_dn", 1, 0), ("on_up", 5), ("on_dn", 5), ("end", 0, 0), ("y_up", 1, 1),
-    ("y_dn", 1, 1), ("update", 3), ("y_up", 0, 1), ("y_dn", 0, 1), ("last", 1, 0), ("update", 4), ("last", 1, 1),
-    ("update", 5), ("last_own", 0, 1), ("end", 1, 0), ("end", 1, 1),
+    ("noise", 10), ("state", 0), ("state", 1), ("state", 2), ("state", 3), ("state_up", 0), ("state_dn", 0),
+    ("token", 0), ("token", 1), ("state_up", 1), ("state_dn", 1), ("token_up", 0), ("token_dn", 0), ("state", 4),
+    ("state_up", 2), ("state_dn", 2), ("token_up", 1), ("token_dn", 1), ("state_up", 3), ("state_dn", 3),
+    ("token_up", 2), ("state", 5), ("noise", 11), ("token_dn", 2), ("noise", 12), ("tokens", 0), ("noise", 13),
+    ("A", 0), ("A", 1), ("state_up", 4), ("state_dn", 4), ("noise", 14), ("A", 2), ("state_up", 5), ("state_dn", 5),
+    ("noise", 15), ("B", 0), ("B", 1), ("noise", 16), ("B", 2), ("noise", 17), ("turn", 0), ("C", 0), ("noise", 18),
+    ("turn", 1), ("C", 1), ("noise", 19), ("A", 3), ("on_up", 0), ("turn", 2), ("C", 2), ("on_dn", 0), ("noise", 21),
+    ("on_up", 1), ("on_dn", 1), ("noise", 24), ("B", 3), ("on_dn", 2), ("A", 4), ("on_up", 2), ("update", 0),
+    ("update", 1), ("A", 5), ("turn", 3), ("C", 3), ("update", 2), ("B", 4), ("B", 5), ("prod_send", 0, 0),
+    ("prod_send", 0, 1), ("prod_send", 0, 2), ("prod_send", 0, 3), ("prod_own", 0, 0), ("prod_own", 0, 1),
+    ("prod_own", 0, 2), ("prod_own", 0, 3), ("y", 0, 0), ("y", 0, 1), ("y", 0, 2), ("x_first", 0, 3), ("turn", 4),
+    ("on_up", 3), ("C", 4), ("turn", 5), ("y_up", 0, 0), ("y_dn", 0, 0), ("prod_send", 1, 0), ("prod_send", 1, 1),
+    ("prod_send", 1, 2), ("y_up", 0, 1), ("y_dn", 0, 1), ("prod_send", 1, 3), ("prod_own", 1, 0), ("prod_own", 1, 1),
+    ("y", 0, 3), ("y_dn", 0, 2), ("y_up", 0, 2), ("y", 1, 0), ("last", 0, 0), ("y", 1, 1), ("prod_own", 1, 2),
+    ("last", 0, 1), ("y", 1, 2), ("prod_own", 1, 3), ("y", 1, 3), ("y_dn", 0, 3), ("y_up", 0, 3), ("on_dn", 3),
+    ("C", 5), ("last", 0, 2), ("end", 0, 0), ("on_dn", 4), ("end", 0, 1), ("y_up", 1, 0), ("y_dn", 1, 0),
+    ("on_up", 4), ("y_up", 1, 1), ("y_dn", 1, 1), ("end", 0, 2), ("y_up", 1, 2), ("y_dn", 1, 2), ("on_up", 5),
+    ("update", 3), ("y_up", 1, 3), ("y_dn", 1, 3), ("last_own", 0, 3), ("last", 1, 0), ("on_dn", 5), ("last", 1, 1),
+    ("last", 1, 2), ("last", 1, 3), ("end", 1, 0), ("update", 4), ("end", 1, 1), ("update", 5), ("end", 1, 2),
+    ("end", 1, 3),
 )
 PARTS = 2
 
@@ -357,11 +362,12 @@
 
     def din_x_first(s, p):
         c_copies[s, p].wait_recv()
+        at_x = X_FIRST.index((s, p))
         f = pl.ds(p * PW, PW)
         for k in range(NY):
             rows = pl.ds(pl.multiple_of(k * 64 + (1 - l) * 32, 32), 32)
-            x_send[pl.ds(k * 32, 32), :] = (c_own[s, rows, f] + c_recv[s, rows, f].astype(F32)).astype(BF)
-        x_copies[s, p] = send(x_send, x_recv, other_l)
+            x_send[at_x, pl.ds(k * 32, 32), :] = (c_own[s, rows, f] + c_recv[s, rows, f].astype(F32)).astype(BF)
+        x_copies[s, p] = send(x_send.at[at_x], x_recv.at[at_x], other_l)
 
     def depth(s, p):
         return 32 if (s, p) in X_FIRST else 64
@@ -372,7 +378,7 @@
             rows = pl.ds(pl.multiple_of(yy(k) * 64 + l * 32, 32), 32)
             there = pl.ds(pl.multiple_of(yy(k) * 32, 32), 32)
             return c_own[s, rows, g] + (
-                c_recv[s, rows, g].astype(F32) + x_recv[there, pl.ds(second * PH, PH)].astype(F32)
+                c_recv[s, rows, g].astype(F32) + x_recv[X_FIRST.index((s, p)), there, pl.ds(second * PH, PH)].astype(F32)
             )
         rows = pl.ds(pl.multiple_of(yy(k) * 64, 64), 64)
         return c_own[s, rows, g] + c_recv[s, rows, g].astype(F32)
@@ -409,10 +415,9 @@
                 part = part + yu_recv[s, p, 1, d].astype(F32) + yd2_recv[s, p, d].astype(F32)
             else:
                 part = part + yd_recv[s, p, 1, d].astype(F32) + yu2_recv[s, p, d].astype(F32)
-            for b in range(PH // BLOCK):
-                block = (p * PW + second * PH) // BLOCK + b
-                there = pl.ds(pl.multiple_of((2 * block + h) * BLOCK, BLOCK), BLOCK)
-                o_buf[:, there] = part[:, b * BLOCK : (b + 1) * BLOCK].astype(BF)
+            first = p * PW + second * PH
+            there = (2 * (first // BLOCK) + h) * BLOCK + first % BLOCK
+            o_buf[:, pl.ds(pl.multiple_of(there, PH), PH)] = part.astype(BF)
 
     def din_last(s, p):
         y_up2[s, p].wait_recv()
@@ -509,8 +514,8 @@
         vm((2, HALF, WIDE), F32),
         *[vm((2, PIECES, 2, 64, PH), BF)] * 4,
         *[vm(piece, BF)] * 4,
-        vm((128, PW), BF),
-        vm((128, PW), BF),
+        vm((len(X_FIRST), 128, PW), BF),
+        vm((len(X_FIRST), 128, PW), BF),
         vm((3, 32, WIDE), BF),
         vm((3, 32, WIDE), BF),
         vm((32, WIDE), F32),

time: 138 us -> 137 us (level)
  no operation moved by 1% of the time
where the time goes in v4:
time: 137 us
  Pallas kernels  136 us (99%)
    pallas_call x1, Pallas kernels, shards(): pl.pallas_call(kernel, out_shape=outs, in_specs=[anywhere] * 6, out_specs...  132 us
    pallas_call x1, Pallas kernels, shards(): pl.pallas_call(settle, grid=(PARTS,), out_shape=outs, in_specs=blocks, ou...  3.8 us

profile of v4, /device:TPU:0, one launch (start us, length us, event | category | flops | bytes accessed | tf_op | source)
XLA Modules:
  0.0 136.7 jit_solution(9512032646202288298)
XLA Ops:
  0.6 132.3 %shard_map.93 = (f32[688,512]{1,0:T(8,128)}, f32[688,512]{1,0:T(8,128)}, f32[688,512]{1,0:T(8,128)}, bf16[32,4096]{1,0:T(8,128)(2,1)}) custom-call(bf16[512,256]{1,0:T(8,128)(2,1)} %tok_in.1, bf16[688,4096]{1,0:T(8,128)(2,1)} %bitcast.10, bf16[688,512]{1,0:T(8,128)(2,1)} %bitcast.17, f32[688,512]{1,0:T(8,128)} %bitcast.11, f32[688,512]{1,0:T(8,128)} %bitcast.12, ...), custom_call_target="tpu_custom_call" | custom-call | flops 8999999488 | bytes 20971520 | tf_op jit(solution)/shard_map/pallas_call | solution.py:529
  132.9 3.8 %shard_map.94 = (f32[688,512]{1,0:T(8,128)}, f32[688,512]{1,0:T(8,128)}, f32[688,512]{1,0:T(8,128)}, bf16[32,4096]{1,0:T(8,128)(2,1)}) custom-call(f32[688,512]{1,0:T(8,128)} %get-tuple-element.12.refs_0_, f32[688,512]{1,0:T(8,128)} %get-tuple-element.13.refs_1_, f32[688,512]{1,0:T(8,128)} %get-tuple-element.14.refs_2_, ...), custom_call_target="tpu_custom_call" | custom-call | bytes 9437184 | tf_op jit(solution)/shard_map/pallas_call | solution.py:541

commit v5 on v4

--- a/solution.py
+++ b/solution.py
@@ -19,27 +19,28 @@
 X_FIRST = ((0, 3),)
 N_SEM = 192
 ORDER = (
-    ("noise", 10), ("state", 0), ("state", 1), ("state", 2), ("state", 3), ("state_up", 0), ("state_dn", 0),
+    ("noise", 9), ("state", 0), ("state", 1), ("state", 2), ("state", 3), ("state_up", 0), ("state_dn", 0),
     ("token", 0), ("token", 1), ("state_up", 1), ("state_dn", 1), ("token_up", 0), ("token_dn", 0), ("state", 4),
-    ("state_up", 2), ("state_dn", 2), ("token_up", 1), ("token_dn", 1), ("state_up", 3), ("state_dn", 3),
-    ("token_up", 2), ("state", 5), ("noise", 11), ("token_dn", 2), ("noise", 12), ("tokens", 0), ("noise", 13),
-    ("A", 0), ("A", 1), ("state_up", 4), ("state_dn", 4), ("noise", 14), ("A", 2), ("state_up", 5), ("state_dn", 5),
-    ("noise", 15), ("B", 0), ("B", 1), ("noise", 16), ("B", 2), ("noise", 17), ("turn", 0), ("C", 0), ("noise", 18),
-    ("turn", 1), ("C", 1), ("noise", 19), ("A", 3), ("on_up", 0), ("turn", 2), ("C", 2), ("on_dn", 0), ("noise", 21),
-    ("on_up", 1), ("on_dn", 1), ("noise", 24), ("B", 3), ("on_dn", 2), ("A", 4), ("on_up", 2), ("update", 0),
-    ("update", 1), ("A", 5), ("turn", 3), ("C", 3), ("update", 2), ("B", 4), ("B", 5), ("prod_send", 0, 0),
-    ("prod_send", 0, 1), ("prod_send", 0, 2), ("prod_send", 0, 3), ("prod_own", 0, 0), ("prod_own", 0, 1),
-    ("prod_own", 0, 2), ("prod_own", 0, 3), ("y", 0, 0), ("y", 0, 1), ("y", 0, 2), ("x_first", 0, 3), ("turn", 4),
-    ("on_up", 3), ("C", 4), ("turn", 5), ("y_up", 0, 0), ("y_dn", 0, 0), ("prod_send", 1, 0), ("prod_send", 1, 1),
-    ("prod_send", 1, 2), ("y_up", 0, 1), ("y_dn", 0, 1), ("prod_send", 1, 3), ("prod_own", 1, 0), ("prod_own", 1, 1),
-    ("y", 0, 3), ("y_dn", 0, 2), ("y_up", 0, 2), ("y", 1, 0), ("last", 0, 0), ("y", 1, 1), ("prod_own", 1, 2),
-    ("last", 0, 1), ("y", 1, 2), ("prod_own", 1, 3), ("y", 1, 3), ("y_dn", 0, 3), ("y_up", 0, 3), ("on_dn", 3),
-    ("C", 5), ("last", 0, 2), ("end", 0, 0), ("on_dn", 4), ("end", 0, 1), ("y_up", 1, 0), ("y_dn", 1, 0),
-    ("on_up", 4), ("y_up", 1, 1), ("y_dn", 1, 1), ("end", 0, 2), ("y_up", 1, 2), ("y_dn", 1, 2), ("on_up", 5),
-    ("update", 3), ("y_up", 1, 3), ("y_dn", 1, 3), ("last_own", 0, 3), ("last", 1, 0), ("on_dn", 5), ("last", 1, 1),
-    ("last", 1, 2), ("last", 1, 3), ("end", 1, 0), ("update", 4), ("end", 1, 1), ("update", 5), ("end", 1, 2),
-    ("end", 1, 3),
+    ("state_up", 2), ("state_dn", 2), ("token_up", 1), ("token_dn", 1), ("noise", 10), ("state_up", 3),
+    ("state_dn", 3), ("noise", 11), ("token_up", 2), ("state", 5), ("noise", 12), ("token_dn", 2), ("noise", 13),
+    ("tokens", 0), ("A", 0), ("A", 1), ("state_up", 4), ("state_dn", 4), ("noise", 14), ("A", 2), ("state_up", 5),
+    ("state_dn", 5), ("noise", 15), ("B", 0), ("B", 1), ("noise", 16), ("B", 2), ("noise", 17), ("turn", 0), ("C", 0),
+    ("noise", 18), ("turn", 1), ("C", 1), ("noise", 19), ("A", 3), ("on_up", 0), ("on_dn", 0), ("turn", 2),
+    ("noise", 20), ("C", 2), ("noise", 22), ("on_up", 1), ("noise", 23), ("on_dn", 1), ("noise", 24), ("update", 0),
+    ("B", 3), ("A", 4), ("on_dn", 2), ("on_up", 2), ("update", 1), ("A", 5), ("turn", 3), ("C", 3), ("update", 2),
+    ("B", 4), ("B", 5), ("prod_send", 0, 0), ("prod_send", 0, 1), ("prod_send", 0, 2), ("prod_send", 0, 3),
+    ("prod_own", 0, 0), ("prod_own", 0, 1), ("prod_own", 0, 2), ("prod_own", 0, 3), ("y", 0, 0), ("y", 0, 1),
+    ("y", 0, 2), ("x_first", 0, 3), ("on_up", 3), ("turn", 4), ("on_dn", 3), ("C", 4), ("y_up", 0, 0), ("y_dn", 0, 0),
+    ("turn", 5), ("prod_send", 1, 0), ("y_up", 0, 1), ("y_dn", 0, 1), ("prod_send", 1, 1), ("prod_send", 1, 2),
+    ("prod_send", 1, 3), ("y_up", 0, 2), ("y_dn", 0, 2), ("y", 0, 3), ("prod_own", 1, 0), ("y", 1, 0),
+    ("prod_own", 1, 1), ("y", 1, 1), ("prod_own", 1, 2), ("y", 1, 2), ("prod_own", 1, 3), ("y", 1, 3), ("y_up", 0, 3),
+    ("y_dn", 0, 3), ("last", 0, 0), ("last", 0, 1), ("last", 0, 2), ("C", 5), ("y_up", 1, 0), ("on_dn", 4),
+    ("y_dn", 1, 0), ("y_up", 1, 1), ("y_dn", 1, 1), ("on_up", 4), ("update", 3), ("end", 0, 0), ("y_up", 1, 2),
+    ("y_dn", 1, 2), ("end", 0, 1), ("end", 0, 2), ("y_up", 1, 3), ("y_dn", 1, 3), ("on_up", 5), ("last_own", 0, 3),
+    ("on_dn", 5), ("last", 1, 0), ("last", 1, 1), ("last", 1, 2), ("last", 1, 3), ("update", 4), ("end", 1, 0),
+    ("update", 5), ("end", 1, 1), ("end", 1, 2), ("end", 1, 3),
 )
+DRAINS = {("turn", 3): ("A", 3), ("end", 1, 0): ("B", 5)}
 PARTS = 2
 
 
@@ -464,7 +465,15 @@
         "x_first": din_x_first, "y": din_y, "y_up": din_y_up, "y_dn": din_y_dn,
         "last": din_last, "last_own": din_last_own, "end": din_end,
     }
-    for name, *where in ORDER:
+    marks, drained = {}, 0
+    for step in ORDER:
+        marks[step] = len(sent)
+        if step in DRAINS:
+            upto = marks[DRAINS[step]]
+            for copy in sent[drained:upto]:
+                copy.wait_send()
+            drained = upto
+        name, *where = step
         steps[name](*where)
     store(o_buf, din_out)
     for copy in stores:
@@ -475,7 +484,7 @@
     def _():
         t_far.wait_send()
 
-    for copy in sent:
+    for copy in sent[drained:]:
         copy.wait_send()
 
 

time: 137 us -> 136 us (level)
  no operation moved by 1% of the time
where the time goes in v5:
time: 136 us
  Pallas kernels  135 us (99%)
    pallas_call x1, Pallas kernels, shards(): pl.pallas_call(kernel, out_shape=outs, in_specs=[anywhere] * 6, out_specs...  132 us
    pallas_call x1, Pallas kernels, shards(): pl.pallas_call(settle, grid=(PARTS,), out_shape=outs, in_specs=blocks, ou...  3.8 us

profile of v5, /device:TPU:0, one launch (start us, length us, event | category | flops | bytes accessed | tf_op | source)
XLA Modules:
  0.0 136.1 jit_solution(13796604501814588985)
XLA Ops:
  0.6 131.6 %shard_map.93 = (f32[688,512]{1,0:T(8,128)}, f32[688,512]{1,0:T(8,128)}, f32[688,512]{1,0:T(8,128)}, bf16[32,4096]{1,0:T(8,128)(2,1)}) custom-call(bf16[512,256]{1,0:T(8,128)(2,1)} %tok_in.1, bf16[688,4096]{1,0:T(8,128)(2,1)} %bitcast.10, bf16[688,512]{1,0:T(8,128)(2,1)} %bitcast.17, f32[688,512]{1,0:T(8,128)} %bitcast.11, f32[688,512]{1,0:T(8,128)} %bitcast.12, ...), custom_call_target="tpu_custom_call" | custom-call | flops 8999999488 | bytes 20971520 | tf_op jit(solution)/shard_map/pallas_call | solution.py:538
  132.3 3.8 %shard_map.94 = (f32[688,512]{1,0:T(8,128)}, f32[688,512]{1,0:T(8,128)}, f32[688,512]{1,0:T(8,128)}, bf16[32,4096]{1,0:T(8,128)(2,1)}) custom-call(f32[688,512]{1,0:T(8,128)} %get-tuple-element.12.refs_0_, f32[688,512]{1,0:T(8,128)} %get-tuple-element.13.refs_1_, f32[688,512]{1,0:T(8,128)} %get-tuple-element.14.refs_2_, ...), custom_call_target="tpu_custom_call" | custom-call | bytes 9437184 | tf_op jit(solution)/shard_map/pallas_call | solution.py:550
